TPU v7x, 256 devices: a whole 4x4x8 slice. The times are simulated.
256 devices in a mesh: ka: 64 (over z, x_hi, y), row: 4 (over x_lo, core).
Axes of the slice: x: 4 (x_hi: 2, x_lo: 2; x = x_hi * 2 + x_lo), y: 4, z: 8, core: 2. Of those that a mesh axis runs over, the one named last changes fastest.
Arguments:
- occupied: bfloat16 [64, 8, 16384], P('ka', None, 'row'), may hold values from -6 to 6
- empty: bfloat16 [64, 64, 16384], P('ka', None, 'row'), may hold values from -6 to 6
- occ_energy: bfloat16 [64, 8], P('ka'), may hold values from -3 to -0.5
- emp_energy: bfloat16 [64, 64], P('ka'), may hold values from 0.5 to 3
- partner: int32 [2, 64], replicated, may hold values from 0 to 63, as said below
- gvecs: int32 [2, 384, 3], replicated, may hold values from -4 to 4
Outputs:
- polarity: float32 [2, 768, 768], P(None, 'ka', 'row')
Inputs may be any that keep to these rules, and one draw needn't show every extreme that they name: partner[q, k] is the index of k + q_q on the periodic 4 x 4 x 4 grid of k-points, k = (i * 4 + j) * 4 + l, where each momentum q_q is a nonzero step along the first dimension only.
All inputs are finite; a program needn't handle non-finite values.
Results may differ from a plain program's by a relative error of at most 0.004.
Values may be sent and summed in bfloat16 or wider, within the bound.
A program may use at most 64 MiB of HBM per device.

v0:
```python
import math

import jax
import jax.numpy as jnp
from jax import lax
from jax.sharding import PartitionSpec as P

GY = 16
GZ = 32


def from_behind(block, axis, distance):
    devices = range(lax.axis_size(axis))
    route = [((i - distance) % len(devices), i) for i in devices]
    return lax.ppermute(block, axis, route)


def in_blocks(array, dim, peers):
    before, after = (array.shape[:dim], array.shape[dim + 1 :])
    return jnp.moveaxis(array.reshape(*before, peers, -1, *after), dim, 0)


def summed_on_arrival(array, axis, dim):
    blocks = in_blocks(array, dim, lax.axis_size(axis))
    arrived = lax.all_to_all(blocks, axis, split_axis=0, concat_axis=0, tiled=True)
    return arrived.sum(axis=0)


def summed_on_arrival_2(array, axis, dim):
    blocks = in_blocks(array, dim, lax.axis_size(axis))
    arrived = lax.all_to_all(blocks, axis, split_axis=0, concat_axis=0, tiled=True)
    return arrived.astype(jnp.float32).sum(axis=0)


def phase_table(plane_waves, start_point, point_count, grid_x, grid_y, grid_z):
    grid_total = grid_x * grid_y * grid_z
    points = start_point + lax.iota(jnp.int32, point_count)
    coord_z = points % grid_z
    coord_y = points // grid_z % grid_y
    coord_x = points // (grid_y * grid_z)
    phase_index = (
        plane_waves[:, 0:1] * coord_x[None, :] * (grid_y * grid_z)
        + plane_waves[:, 1:2] * coord_y[None, :] * (grid_x * grid_z)
        + plane_waves[:, 2:3] * coord_z[None, :] * (grid_x * grid_y)
    ) % grid_total
    angle = phase_index.astype(jnp.float32) * (2.0 * math.pi / grid_total)
    return jnp.concatenate([jnp.cos(angle), jnp.sin(angle)], axis=0).astype(jnp.bfloat16)


def plane_stride():
    kpoint_count = lax.axis_size("ka")
    return kpoint_count // min(4, kpoint_count)


def fetch_occupied(block, levels, count):
    stride = plane_stride()

    def advance(index, carry):
        return from_behind((carry[0], carry[1]), "ka", stride)

    return lax.fori_loop(0, count, advance, (block, levels))


def per_device(occupied, empty, occ_energy, emp_energy, partner, gvecs):
    stride = plane_stride()
    row_count = lax.axis_size("row")
    point_rows = occupied.shape[2]
    grid_points = point_rows * row_count
    grid_x = grid_points // (GY * GZ)
    start_point = lax.axis_index("row") * point_rows
    pair_count = occupied.shape[1] * empty.shape[1]
    pair_width = pair_count // row_count
    results = []
    for moment in range(partner.shape[0]):
        steps_taken = partner[moment, 0] // stride
        occ_block, occ_level = fetch_occupied(occupied, occ_energy, steps_taken)
        emp_block, emp_level = (empty, emp_energy)
        density = (
            (
                occ_block[0].astype(jnp.float32)[:, None, :]
                * emp_block[0].astype(jnp.float32)[None, :, :]
            )
            .reshape(pair_count, point_rows)
            .astype(jnp.bfloat16)
        )
        table_q = phase_table(gvecs[moment], start_point, point_rows, grid_x, GY, GZ)
        partial_value = lax.dot_general(
            density, table_q, (((1,), (1,)), ((), ())), preferred_element_type=jnp.float32
        )
        weight = (
            1.0
            / (
                emp_level[0].astype(jnp.float32)[None, :]
                - occ_level[0].astype(jnp.float32)[:, None]
            )
        ).reshape(pair_count)
        owned = summed_on_arrival(partial_value, "row", 0) * (1.0 / grid_points)
        own_weight = lax.dynamic_slice_in_dim(
            weight, lax.axis_index("row") * pair_width, pair_width, 0
        )
        left_side = owned.astype(jnp.bfloat16)
        right_side = (own_weight[:, None] * owned).astype(jnp.bfloat16)
        full_part = lax.dot_general(
            left_side, right_side, (((0,), (0,)), ((), ())), preferred_element_type=jnp.float32
        )
        gram_part = summed_on_arrival_2(full_part.astype(jnp.bfloat16), "row", 1)
        results.append(gram_part)
    return summed_on_arrival(jnp.stack(results), "ka", 1)


def solution(mesh):
    placed = (P("ka", None, "row"), P("ka", None, "row"), P("ka", None), P("ka", None), P(), P())
    return jax.shard_map(
        per_device, mesh=mesh, in_specs=placed, out_specs=P(None, "ka", "row"), check_vma=False
    )
```

profile of v0, /device:TPU:1, one launch (start us, length us, event | category | flops | bytes accessed | tf_op | source)
XLA Modules:
  0.0 243.5 jit_solution(15202146968965158580)
XLA Ops:
  0.0 0.7 copy.36
  0.7 0.8 copy.35
  1.5 1.3 fusion.28
  7.7 0.8 fusion.27
  8.6 1.1 bitcast_convert_fusion
  9.7 8.9 %while.25 = (s32[]{:T(128)}, bf16[1,8,4096]{2,1,0:T(8,128)(2,1)S(1)}, bf16[1,8]{1,0:T(2,128)(2,1)S(1)}, s32[]{:T(128)}, s32[]{:T(128)}) while((s32[]{:T(128)}, bf16[1,8,4096]{2,1,0:T(8,128)(2,1)S(1)}, bf16[1,8]{1,0:T(2,128)(2,1)S(1)}, s32[]{:T(128)}, s32[]{:T(128)}) %tuple.47), condition=%wide.region_5.6_spmd, body=%wide.region_4.5_spmd.sunk | while | flops 2 | bytes 393453 | solution.py:61
  9.7 3.9 %collective-permute-start.2 = (bf16[1,8,4096]{2,1,0:T(8,128)(2,1)S(1)}, bf16[1,8,4096]{2,1,0:T(8,128)(2,1)S(1)}, u32[]{:S(2)}, u32[]{:S(2)}) collective-permute-start(bf16[1,8,4096]{2,1,0:T(8,128)(2,1)S(1)} %get-tuple-element.159), channel_id=1, source_target_pairs={{192,0},{196,4},{200,8},{204,12},{208,16},{212,20},{216,24},{220,2... | collective-permute-start | bytes 196616 | tf_op jit(solution)/shard_map/while/body/ppermute | solution.py:15
  13.6 4.2 %collective-permute-start.3 = (bf16[1,8]{1,0:T(2,128)(2,1)S(1)}, bf16[1,8]{1,0:T(2,128)(2,1)S(1)}, u32[]{:S(2)}, u32[]{:S(2)}) collective-permute-start(bf16[1,8]{1,0:T(2,128)(2,1)S(1)} %get-tuple-element.160), channel_id=1, source_target_pairs={{192,0},{196,4},{200,8},{204,12},{208,16},{212,20},{216,24},{220,2... | collective-permute-start | bytes 56 | tf_op jit(solution)/shard_map/while/body/ppermute | solution.py:15
  17.8 0.7 collective-permute-done.3
  18.5 0.0 collective-permute-done.2
  18.6 19.6 %while.24 = (s32[]{:T(128)}, bf16[1,8,4096]{2,1,0:T(8,128)(2,1)S(1)}, bf16[1,8]{1,0:T(2,128)(2,1)S(1)}, s32[]{:T(128)}, s32[]{:T(128)}) while((s32[]{:T(128)}, bf16[1,8,4096]{2,1,0:T(8,128)(2,1)S(1)}, bf16[1,8]{1,0:T(2,128)(2,1)S(1)}, s32[]{:T(128)}, s32[]{:T(128)}) %tuple.50), condition=%wide.region_1.2_spmd, body=%wide.region_0.1_spmd.sunk | while | flops 2 | bytes 393453 | solution.py:61
  18.6 2.6 %collective-permute-start = (bf16[1,8,4096]{2,1,0:T(8,128)(2,1)S(1)}, bf16[1,8,4096]{2,1,0:T(8,128)(2,1)S(1)}, u32[]{:S(2)}, u32[]{:S(2)}) collective-permute-start(bf16[1,8,4096]{2,1,0:T(8,128)(2,1)S(1)} %get-tuple-element.174), channel_id=1, source_target_pairs={{192,0},{196,4},{200,8},{204,12},{208,16},{212,20},{216,24},{220,2... | collective-permute-start | bytes 196616 | tf_op jit(solution)/shard_map/while/body/ppermute | solution.py:15
  21.2 3.2 %collective-permute-start.1 = (bf16[1,8]{1,0:T(2,128)(2,1)S(1)}, bf16[1,8]{1,0:T(2,128)(2,1)S(1)}, u32[]{:S(2)}, u32[]{:S(2)}) collective-permute-start(bf16[1,8]{1,0:T(2,128)(2,1)S(1)} %get-tuple-element.175), channel_id=1, source_target_pairs={{192,0},{196,4},{200,8},{204,12},{208,16},{212,20},{216,24},{220,2... | collective-permute-start | bytes 56 | tf_op jit(solution)/shard_map/while/body/ppermute | solution.py:15
  24.4 1.6 collective-permute-done.1
  26.0 0.0 collective-permute-done
  26.1 2.0 collective-permute-start
  28.1 1.7 collective-permute-start.1
  29.8 2.8 %collective-permute-done.1 = bf16[1,8]{1,0:T(2,128)(2,1)S(1)} collective-permute-done((bf16[1,8]{1,0:T(2,128)(2,1)S(1)}, bf16[1,8]{1,0:T(2,128)(2,1)S(1)}, u32[]{:S(2)}, u32[]{:S(2)}) %collective-permute-start.1) | collective-permute-done | bytes 48 | tf_op jit(solution)/shard_map/while/body/ppermute | solution.py:15
  32.6 0.0 collective-permute-done
  32.6 0.6 collective-permute-start
  33.2 2.2 collective-permute-start.1
  35.4 2.6 %collective-permute-done.1 = bf16[1,8]{1,0:T(2,128)(2,1)S(1)} collective-permute-done((bf16[1,8]{1,0:T(2,128)(2,1)S(1)}, bf16[1,8]{1,0:T(2,128)(2,1)S(1)}, u32[]{:S(2)}, u32[]{:S(2)}) %collective-permute-start.1) | collective-permute-done | bytes 48 | tf_op jit(solution)/shard_map/while/body/ppermute | solution.py:15
  38.0 0.0 collective-permute-done
  38.2 3.9 %multiply_convert_fusion.1 = (bf16[8,64,4096]{2,1,0:T(8,128)(2,1)}, bf16[8,64,4096]{2,1,0:T(8,128)(2,1)S(1)}) fusion(f32[64,4096]{1,0:T(8,128)S(1)} %bitcast_convert_fusion, f32[8,4096]{1,0:T(8,128)S(1)} %get-tuple-element.94, f32[8,4096]{1,0:T(8,128)S(1)} %get-tuple-element.93), kind=kLoop, calls=%fused_computation.7 | loop fusion | flops 8388608 | bytes 9699328 | tf_op jit(solution)/shard_map/convert_element_type | solution.py:84
  42.1 54.2 %cosine_convert_fusion.1 = (bf16[384,4096]{1,0:T(8,128)(2,1)}, bf16[384,4096]{1,0:T(8,128)(2,1)}, bf16[384,4096]{1,0:T(8,128)(2,1)S(1)}, bf16[384,4096]{1,0:T(8,128)(2,1)S(1)}) fusion(s32[4096]{0:T(1024)S(1)} %get-tuple-element.95, s32[384]{0:T(512)S(1)} %get-tuple-element.58, s32[4096]{0:T(1024)S(1)} %get-tuple-element.96, s32[384]{0:T(512)S(1)} %get-tuple-element.59, ...), kind=kLoop, calls=%fused_computation.25 | loop fusion | flops 72351744 | bytes 12641280 | tf_op jit(solution)/shard_map/convert.8
  96.2 4.7 %fusion.9 = f32[4,128,768]{2,1,0:T(8,128)} fusion(bf16[4,128,4096]{2,1,0:T(8,128)(2,1)S(1)} %bitcast.44, bf16[384,4096]{1,0:T(8,128)(2,1)S(1)} %get-tuple-element.85, bf16[384,4096]{1,0:T(8,128)(2,1)S(1)} %get-tuple-element.86), kind=kOutput, calls=%fused_computation.19 | convolution fusion | flops 3233808384 | bytes 12058624 | tf_op jit(solution)/shard_map/dot_general | solution.py:87
  100.9 9.4 %all-to-all-start.2 = ((f32[4,128,768]{2,1,0:T(8,128)}), f32[4,128,768]{2,1,0:T(8,128)S(1)}, u32[]{:S(2)}, u32[]{:S(2)}) async-start(f32[4,128,768]{2,1,0:T(8,128)} %fusion.9), calls=%async_computation.2 | async-start | bytes 3145728 | tf_op jit(solution)/shard_map/all_to_all | solution.py:25
  110.3 0.0 copy-start
  110.3 8.7 %fusion.6 = f32[4,128,768]{2,1,0:T(8,128)} fusion(bf16[4,128,4096]{2,1,0:T(8,128)(2,1)} %bitcast.43, bf16[384,4096]{1,0:T(8,128)(2,1)} %get-tuple-element.82, bf16[384,4096]{1,0:T(8,128)(2,1)} %get-tuple-element.81), kind=kOutput, calls=%fused_computation.15 | convolution fusion | flops 3233808384 | bytes 12058624 | tf_op jit(solution)/shard_map/dot_general | solution.py:87
  119.0 10.5 %all-to-all-done.2 = f32[4,128,768]{2,1,0:T(8,128)S(1)} async-done(((f32[4,128,768]{2,1,0:T(8,128)}), f32[4,128,768]{2,1,0:T(8,128)S(1)}, u32[]{:S(2)}, u32[]{:S(2)}) %all-to-all-start.2) | async-done | bytes 1572896 | tf_op jit(solution)/shard_map/all_to_all | solution.py:25
  129.5 4.4 %all-to-all-start = ((f32[4,128,768]{2,1,0:T(8,128)}), f32[4,128,768]{2,1,0:T(8,128)S(1)}, u32[]{:S(2)}, u32[]{:S(2)}) async-start(f32[4,128,768]{2,1,0:T(8,128)} %fusion.6), calls=%async_computation | async-start | bytes 3145728 | tf_op jit(solution)/shard_map/all_to_all | solution.py:25
  133.9 0.0 copy-done
  133.9 0.1 subtract_divide_fusion.1
  134.0 0.1 div.72
  134.1 0.1 dynamic-slice_multiply_fusion
  134.2 0.1 reduce_sum.47
  134.3 1.6 convolution_convert_fusion
  135.9 17.2 %all-to-all-done = f32[4,128,768]{2,1,0:T(8,128)S(1)} async-done(((f32[4,128,768]{2,1,0:T(8,128)}), f32[4,128,768]{2,1,0:T(8,128)S(1)}, u32[]{:S(2)}, u32[]{:S(2)}) %all-to-all-start) | async-done | bytes 1572896 | tf_op jit(solution)/shard_map/all_to_all | solution.py:25
  153.1 4.4 %all-to-all-start.3 = ((bf16[4,768,192]{1,2,0:T(8,128)(2,1)}), bf16[4,768,192]{1,2,0:T(8,128)(2,1)S(1)}, u32[]{:S(2)}, u32[]{:S(2)}) async-start(bf16[4,768,192]{1,2,0:T(8,128)(2,1)} %bitcast.42), calls=%async_computation.3 | async-start | bytes 2359296 | tf_op jit(solution)/shard_map/all_to_all | solution.py:31
  157.5 0.1 div.67
  157.6 0.1 dynamic-slice_multiply_fusion.1
  157.6 0.1 reduce_sum.45
  157.8 1.6 convolution_convert_fusion.1
  159.4 13.1 %all-to-all-done.3 = bf16[4,768,192]{1,2,0:T(8,128)(2,1)S(1)} async-done(((bf16[4,768,192]{1,2,0:T(8,128)(2,1)}), bf16[4,768,192]{1,2,0:T(8,128)(2,1)S(1)}, u32[]{:S(2)}, u32[]{:S(2)}) %all-to-all-start.3) | async-done | bytes 1179680 | tf_op jit(solution)/shard_map/all_to_all | solution.py:31
  172.5 4.4 %all-to-all-start.1 = ((bf16[4,768,192]{1,2,0:T(8,128)(2,1)}), bf16[4,768,192]{1,2,0:T(8,128)(2,1)S(1)}, u32[]{:S(2)}, u32[]{:S(2)}) async-start(bf16[4,768,192]{1,2,0:T(8,128)(2,1)} %bitcast.8), calls=%async_computation.1 | async-start | bytes 2359296 | tf_op jit(solution)/shard_map/all_to_all | solution.py:31
  176.9 1.0 convert_reduce_fusion
  177.9 1.3 copy.8
  179.2 0.1 stack.10
  179.3 12.6 %all-to-all-done.1 = bf16[4,768,192]{1,2,0:T(8,128)(2,1)S(1)} async-done(((bf16[4,768,192]{1,2,0:T(8,128)(2,1)}), bf16[4,768,192]{1,2,0:T(8,128)(2,1)S(1)}, u32[]{:S(2)}, u32[]{:S(2)}) %all-to-all-start.1) | async-done | bytes 1179680 | tf_op jit(solution)/shard_map/all_to_all | solution.py:31
  191.9 1.0 convert_reduce_fusion.1
  192.8 1.3 copy.7
  194.2 0.1 stack.9
  194.3 0.2 maximum_bitcast_fusion.4
  194.5 1.4 copy.9
  195.9 46.4 %all_to_all.25 = f32[64,2,12,192]{3,1,2,0:T(2,128)S(1)} all-to-all(f32[64,2,12,192]{3,1,2,0:T(2,128)S(1)} %copy.9), channel_id=1, replica_groups=mesh['ka'=64,'row'=4] {'ka'}, dimensions={0} | all-to-all | bytes 2359296 | tf_op jit(solution)/shard_map/all_to_all | solution.py:25
  242.3 1.2 reduce_sum.49
  (18 shorter events, 0.2 us)
Async XLA Ops:
  9.7 8.8 %collective-permute-start.2 = (bf16[1,8,4096]{2,1,0:T(8,128)(2,1)S(1)}, bf16[1,8,4096]{2,1,0:T(8,128)(2,1)S(1)}, u32[]{:S(2)}, u32[]{:S(2)}) collective-permute-start(bf16[1,8,4096]{2,1,0:T(8,128)(2,1)S(1)} %get-tuple-element.159), channel_id=1, source_target_pairs={{192,0},{196,4},{200,8},{204,12},{208,16},{212,20},{216,24},{220,2... | collective-permute-start | bytes 196616 | tf_op jit(solution)/shard_map/while/body/ppermute | solution.py:15
  13.6 4.9 %collective-permute-start.3 = (bf16[1,8]{1,0:T(2,128)(2,1)S(1)}, bf16[1,8]{1,0:T(2,128)(2,1)S(1)}, u32[]{:S(2)}, u32[]{:S(2)}) collective-permute-start(bf16[1,8]{1,0:T(2,128)(2,1)S(1)} %get-tuple-element.160), channel_id=1, source_target_pairs={{192,0},{196,4},{200,8},{204,12},{208,16},{212,20},{216,24},{220,2... | collective-permute-start | bytes 56 | tf_op jit(solution)/shard_map/while/body/ppermute | solution.py:15
  18.6 7.5 %collective-permute-start = (bf16[1,8,4096]{2,1,0:T(8,128)(2,1)S(1)}, bf16[1,8,4096]{2,1,0:T(8,128)(2,1)S(1)}, u32[]{:S(2)}, u32[]{:S(2)}) collective-permute-start(bf16[1,8,4096]{2,1,0:T(8,128)(2,1)S(1)} %get-tuple-element.174), channel_id=1, source_target_pairs={{192,0},{196,4},{200,8},{204,12},{208,16},{212,20},{216,24},{220,2... | collective-permute-start | bytes 196616 | tf_op jit(solution)/shard_map/while/body/ppermute | solution.py:15
  21.2 4.8 %collective-permute-start.1 = (bf16[1,8]{1,0:T(2,128)(2,1)S(1)}, bf16[1,8]{1,0:T(2,128)(2,1)S(1)}, u32[]{:S(2)}, u32[]{:S(2)}) collective-permute-start(bf16[1,8]{1,0:T(2,128)(2,1)S(1)} %get-tuple-element.175), channel_id=1, source_target_pairs={{192,0},{196,4},{200,8},{204,12},{208,16},{212,20},{216,24},{220,2... | collective-permute-start | bytes 56 | tf_op jit(solution)/shard_map/while/body/ppermute | solution.py:15
  26.1 6.5 %collective-permute-start = (bf16[1,8,4096]{2,1,0:T(8,128)(2,1)S(1)}, bf16[1,8,4096]{2,1,0:T(8,128)(2,1)S(1)}, u32[]{:S(2)}, u32[]{:S(2)}) collective-permute-start(bf16[1,8,4096]{2,1,0:T(8,128)(2,1)S(1)} %get-tuple-element.174), channel_id=1, source_target_pairs={{192,0},{196,4},{200,8},{204,12},{208,16},{212,20},{216,24},{220,2... | collective-permute-start | bytes 196616 | tf_op jit(solution)/shard_map/while/body/ppermute | solution.py:15
  28.1 4.5 %collective-permute-start.1 = (bf16[1,8]{1,0:T(2,128)(2,1)S(1)}, bf16[1,8]{1,0:T(2,128)(2,1)S(1)}, u32[]{:S(2)}, u32[]{:S(2)}) collective-permute-start(bf16[1,8]{1,0:T(2,128)(2,1)S(1)} %get-tuple-element.175), channel_id=1, source_target_pairs={{192,0},{196,4},{200,8},{204,12},{208,16},{212,20},{216,24},{220,2... | collective-permute-start | bytes 56 | tf_op jit(solution)/shard_map/while/body/ppermute | solution.py:15
  32.6 5.4 %collective-permute-start = (bf16[1,8,4096]{2,1,0:T(8,128)(2,1)S(1)}, bf16[1,8,4096]{2,1,0:T(8,128)(2,1)S(1)}, u32[]{:S(2)}, u32[]{:S(2)}) collective-permute-start(bf16[1,8,4096]{2,1,0:T(8,128)(2,1)S(1)} %get-tuple-element.174), channel_id=1, source_target_pairs={{192,0},{196,4},{200,8},{204,12},{208,16},{212,20},{216,24},{220,2... | collective-permute-start | bytes 196616 | tf_op jit(solution)/shard_map/while/body/ppermute | solution.py:15
  33.2 4.8 %collective-permute-start.1 = (bf16[1,8]{1,0:T(2,128)(2,1)S(1)}, bf16[1,8]{1,0:T(2,128)(2,1)S(1)}, u32[]{:S(2)}, u32[]{:S(2)}) collective-permute-start(bf16[1,8]{1,0:T(2,128)(2,1)S(1)} %get-tuple-element.175), channel_id=1, source_target_pairs={{192,0},{196,4},{200,8},{204,12},{208,16},{212,20},{216,24},{220,2... | collective-permute-start | bytes 56 | tf_op jit(solution)/shard_map/while/body/ppermute | solution.py:15
  100.9 28.6 %all-to-all-start.2 = ((f32[4,128,768]{2,1,0:T(8,128)}), f32[4,128,768]{2,1,0:T(8,128)S(1)}, u32[]{:S(2)}, u32[]{:S(2)}) async-start(f32[4,128,768]{2,1,0:T(8,128)} %fusion.9), calls=%async_computation.2 | async-start | bytes 3145728 | tf_op jit(solution)/shard_map/all_to_all | solution.py:25
  110.3 23.6 %copy-start = (bf16[1,64]{1,0:T(2,128)(2,1)S(1)}, bf16[1,64]{1,0:T(2,128)(2,1)}, u32[]{:S(2)}) copy-start(bf16[1,64]{1,0:T(2,128)(2,1)} %param.13) | copy-start | bytes 388
  129.5 23.6 %all-to-all-start = ((f32[4,128,768]{2,1,0:T(8,128)}), f32[4,128,768]{2,1,0:T(8,128)S(1)}, u32[]{:S(2)}, u32[]{:S(2)}) async-start(f32[4,128,768]{2,1,0:T(8,128)} %fusion.6), calls=%async_computation | async-start | bytes 3145728 | tf_op jit(solution)/shard_map/all_to_all | solution.py:25
  153.1 19.4 %all-to-all-start.3 = ((bf16[4,768,192]{1,2,0:T(8,128)(2,1)}), bf16[4,768,192]{1,2,0:T(8,128)(2,1)S(1)}, u32[]{:S(2)}, u32[]{:S(2)}) async-start(bf16[4,768,192]{1,2,0:T(8,128)(2,1)} %bitcast.42), calls=%async_computation.3 | async-start | bytes 2359296 | tf_op jit(solution)/shard_map/all_to_all | solution.py:31
  172.5 19.4 %all-to-all-start.1 = ((bf16[4,768,192]{1,2,0:T(8,128)(2,1)}), bf16[4,768,192]{1,2,0:T(8,128)(2,1)S(1)}, u32[]{:S(2)}, u32[]{:S(2)}) async-start(bf16[4,768,192]{1,2,0:T(8,128)(2,1)} %bitcast.8), calls=%async_computation.1 | async-start | bytes 2359296 | tf_op jit(solution)/shard_map/all_to_all | solution.py:31
where the time goes:
time: 247 us; the launch traced here: 243 us
  other arithmetic  63 us (26%)
  waiting for transfers between devices  61.3 us (25%)
  blocking collectives  46.4 us (19%)
  starting transfers between devices  42.9 us (17%)
  matrix products  16.6 us (7%)
  local copies, waits for them, and re-layouts  8.1 us (3%)
  between operations  4.99 us (2%)
    another operation x1, other arithmetic  54.2 us
    all_to_all x1, blocking collectives, summed_on_arrival(): lax.all_to_all(blocks, axis, split_axis=0, concat_axis=0, tiled=True)  46.4 us
    all_to_all x2, waiting for transfers between devices, summed_on_arrival(): lax.all_to_all(blocks, axis, split_axis=0, concat_axis=0, tiled=True)  27.8 us
    all_to_all x2, waiting for transfers between devices, summed_on_arrival_2(): lax.all_to_all(blocks, axis, split_axis=0, concat_axis=0, tiled=True)  25.7 us
    ppermute x8, starting transfers between devices, from_behind(): return lax.ppermute(block, axis, route)  20.4 us
    all_to_all x2, starting transfers between devices, summed_on_arrival(): lax.all_to_all(blocks, axis, split_axis=0, concat_axis=0, tiled=True)  13.8 us
    dot_general x2, matrix products, per_device(): lax.dot_general(density, table_q, (((1,), (1,)), ((), ())), preferred_ele...  13.3 us
    all_to_all x2, starting transfers between devices, summed_on_arrival_2(): lax.all_to_all(blocks, axis, split_axis=0, concat_axis=0, tiled=True)  8.73 us
  transfers between devices with their start and end apart: 12, of which 8 were waited for; matrix products, arithmetic and copies ran while one was open for 6% of the time, Pallas kernels for 0%

commit v1 on v0

v1 whole, which is shorter than its diff:
```python
import math

import jax
import jax.numpy as jnp
import numpy as np
from jax import lax
from jax.experimental import pallas as pl
from jax.experimental.pallas import tpu as pltpu
from jax.sharding import PartitionSpec as P

MESH = pl.DeviceIdType.MESH
F32 = jnp.float32
BF16 = jnp.bfloat16
NO = 8
NB = 32
NG = 384
PTS = 4096
YZ = 512
GY = 16
GZ = 32
NX = 8
COLS = 2 * NG


def yz_table():
    point = np.arange(YZ)
    y, z = point // GZ, point % GZ
    table = np.zeros((YZ, 128), np.float64)
    for g1 in range(-4, 5):
        for g2 in range(5):
            turn = 2 * math.pi * ((g1 * y * 2 + g2 * z) % 32) / 32
            column = (g1 + 4) * 5 + g2
            table[:, column] = np.cos(turn)
            table[:, 64 + column] = np.sin(turn)
    return table.astype(np.float32)


def row_order():
    a = np.arange(COLS)
    z, xh, y, i = a // 96, a // 48 % 2, a // 12 % 4, a % 12
    first = xh * 192 + y * 48 + (z % 4) * 12 + i
    second = 384 + y * 96 + xh * 48 + (z % 4) * 12 + i
    return np.where(z < 4, first, second).astype(np.int32)


def kernel(
    occ_ref, emp_ref, oe_ref, ee_ref, partner_ref, wave_ref, yz_ref, out_ref,
    shift, oe_src, oe_shift, efull, osel, ofull, wtab, utab, vtab, ybuf, proj, gram,
    ra1, rb1, sa2, sb2, ra2, rb2, sa3, sb3, st3, r3,
    zsend, zrecv, gsend, grecv, rsend, rrecv, fsend, frecv, lsem,
):
    ka, row = lax.axis_index("ka"), lax.axis_index("row")
    z, xh, y = ka // 8, ka // 4 % 2, ka % 4
    xl, core = row // 2, row % 2
    x = xh * 2 + xl

    def device(z_, x_, y_, core_):
        return (z_ * 8 + (x_ // 2) * 4 + y_, (x_ % 2) * 2 + core_)

    sibling = (ka, xl * 2 + 1 - core)
    across = (ka, (1 - xl) * 2 + core)
    diagonal = (ka, (1 - xl) * 2 + 1 - core)
    x_peer = [device(z, (x + d) % 4, y, core) for d in range(1, 4)]
    y_peer = [device(z, x, (y + d) % 4, core) for d in range(1, 4)]
    z_peer = [[device((z + d) % 8, x, y, core if r == 0 else 1 - core) for r in range(2)] for d in range(8)]

    barrier = pltpu.get_barrier_semaphore()
    peers = [sibling, across, diagonal] + x_peer + y_peer + [z_peer[d][r] for d in range(1, 8) for r in range(2)]
    for peer in peers:
        pl.semaphore_signal(barrier, inc=1, device_id=peer, device_id_type=MESH)

    eye = lax.broadcasted_iota(jnp.int32, (NO, NO), 0) == lax.broadcasted_iota(jnp.int32, (NO, NO), 1)
    levels = jnp.broadcast_to(oe_ref[...].astype(F32), (NO, NO))
    column = jnp.sum(jnp.where(eye, levels, 0.0), axis=1, keepdims=True)
    oe_src[...] = jnp.broadcast_to(column, (NO, 128))
    pl.semaphore_wait(barrier, len(peers))

    def send(src, dst, sends, recvs, index, peer):
        copy = pltpu.make_async_remote_copy(
            src_ref=src, dst_ref=dst, send_sem=sends.at[index], recv_sem=recvs.at[index],
            device_id=peer, device_id_type=MESH,
        )
        copy.start()
        return copy

    shifts = []
    for s in range(1, 4):
        shifts.append(send(occ_ref.at[0], shift.at[s - 1], zsend, zrecv, s - 1, z_peer[2 * s][0]))
        shifts.append(send(oe_src, oe_shift.at[s - 1], zsend, zrecv, s + 2, z_peer[2 * s][0]))
    theirs = []
    for part in range(2):
        bands = pl.ds(pl.multiple_of((1 - xl) * NB + part * 16, 16), 16)
        theirs.append(send(emp_ref.at[0, bands], efull.at[2, pl.ds(part * 16, 16)], gsend, grecv, part, across))
    own_bands = pl.ds(pl.multiple_of(xl * NB, NB), NB)
    beside = send(emp_ref.at[0, own_bands], efull.at[1], gsend, grecv, 2, sibling)
    local = pltpu.make_async_copy(emp_ref.at[0, own_bands], efull.at[0], lsem)
    local.start()

    wave = wave_ref[core]
    g0, g1, g2, order = wave[0:1], wave[1:2], wave[2:3], wave[3:4]
    flip = jnp.where(g2 < 0, -1, 1)
    group = (flip * g1 + 4) * 5 + flip * g2
    slot_x = lax.broadcasted_iota(jnp.int32, (4 * NX, COLS), 0)
    other_core, other_xl = (slot_x // NX) % 2, slot_x // (2 * NX)
    src_core = core + other_core - 2 * core * other_core
    src_xl = xl + other_xl - 2 * xl * other_xl
    plane = (src_xl * 2 + src_core) * NX + slot_x % NX
    quarter = jnp.where(lax.broadcasted_iota(jnp.int32, (4 * NX, COLS), 1) < NG, 0, 8)
    turn = ((g0 * plane - quarter) & 31).astype(F32) * (2.0 * math.pi / 32)
    utab[...] = jnp.cos(turn)
    vtab[...] = jnp.sin(turn) * (-flip).astype(F32)
    chosen = lax.broadcasted_iota(jnp.int32, (64, COLS), 0) == group

    for slot in range(4):
        def fill(i, carry):
            u = utab[pl.ds(slot * NX + i, 1), :]
            v = vtab[pl.ds(slot * NX + i, 1), :]
            base = pl.multiple_of(i * 128, 128)
            wtab[slot, pl.ds(base, 64), :] = jnp.where(chosen, u, 0.0).astype(BF16)
            wtab[slot, pl.ds(base + 64, 64), :] = jnp.where(chosen, v, 0.0).astype(BF16)
            return carry

        lax.fori_loop(0, NX, fill, 0)

    theirs[0].wait_recv()
    passed = [send(efull.at[2, pl.ds(0, 16)], efull.at[3, pl.ds(0, 16)], gsend, grecv, 3, sibling)]
    for copy in shifts:
        copy.wait_recv()
    steps = [jnp.clip(partner_ref[q, 0] // 16, 1, 3) - 1 for q in range(2)]
    for q in range(2):
        osel[q] = shift[steps[q]]
    gathers = [
        send(osel.at[core], ofull.at[2], gsend, grecv, 6, across),
        send(osel.at[1 - core], ofull.at[3], gsend, grecv, 7, diagonal),
        send(osel.at[1 - core], ofull.at[1], gsend, grecv, 5, sibling),
    ]
    ofull[0] = osel[core]
    theirs[1].wait_recv()
    passed.append(send(efull.at[2, pl.ds(16, 16)], efull.at[3, pl.ds(16, 16)], gsend, grecv, 4, sibling))

    oe = jnp.where(core == 0, oe_shift[steps[0]], oe_shift[steps[1]])
    pick = lax.broadcasted_iota(jnp.int32, (NB, 2 * NB), 1) == lax.broadcasted_iota(jnp.int32, (NB, 2 * NB), 0) + xl * NB
    ee = jnp.broadcast_to(ee_ref[...].astype(F32), (NB, 2 * NB))
    ee = jnp.sum(jnp.where(pick, ee, 0.0), axis=1, keepdims=True)
    weight = jnp.concatenate([1.0 / (ee - oe[v : v + 1, 0:1]) for v in range(NO)], axis=0)

    for slot in range(4):
        if slot == 0:
            local.wait()
        elif slot == 1:
            beside.wait_recv()
            gathers[2].wait_recv()
        elif slot == 2:
            gathers[0].wait_recv()
        else:
            gathers[1].wait_recv()
            passed[0].wait_recv()
            passed[1].wait_recv()

        def project(i, carry):
            lanes = pl.ds(pl.multiple_of(i * YZ, YZ), YZ)
            e = efull[slot, :, lanes].astype(F32)
            o = ofull[slot, :, lanes].astype(F32)
            density = jnp.concatenate([(o[v : v + 1] * e).astype(BF16) for v in range(NO)], axis=0)
            part = jnp.dot(density, yz_ref[...], preferred_element_type=F32)
            ybuf[:, pl.ds(pl.multiple_of(i * 128, 128), 128)] = part.astype(BF16)
            return carry

        lax.fori_loop(0, NX, project, 0)
        term = jnp.dot(ybuf[...], wtab[slot], preferred_element_type=F32)
        proj[...] = term if slot == 0 else proj[...] + term

    value = proj[...] * (1.0 / (4 * PTS))
    left = value.astype(BF16)
    right = (weight * value).astype(BF16)
    ordering = jnp.where(lax.broadcasted_iota(jnp.int32, (COLS, COLS), 0) == order, 1.0, 0.0).astype(BF16)
    left_t = lax.dot_general(ordering, left, (((1,), (1,)), ((), ())), preferred_element_type=F32).astype(BF16)
    gram[...] = jnp.dot(left_t, right, preferred_element_type=F32).astype(BF16)

    def a_block(x_):
        return pl.ds(pl.multiple_of(x_ // 2 * 192, 192), 192), pl.ds(pl.multiple_of(x_ % 2 * 384, 384), 384)

    def b_block(y_):
        return pl.ds(pl.multiple_of(384 + y_ * 96, 96), 96)

    first_a, first_b = [], []
    for d in (2, 1, 3):
        rows, cols = a_block((x + d) % 4)
        first_a.append(send(gram.at[rows, cols], ra1.at[d - 1], rsend, rrecv, d - 1, x_peer[d - 1]))
        first_b.append(send(gram.at[b_block((y + d) % 4)], rb1.at[d - 1], rsend, rrecv, d + 2, y_peer[d - 1]))
    for copy in first_a:
        copy.wait_recv()
    rows, cols = a_block(x)
    total = gram[rows, cols].astype(F32)
    for d in range(3):
        total = total + ra1[d].astype(F32)
    sa2[...] = total.astype(BF16)
    second = []
    for d in (2, 1, 3):
        part = pl.ds(pl.multiple_of((y + d) % 4 * 48, 48), 48)
        second.append(send(sa2.at[part], ra2.at[d - 1], rsend, rrecv, d + 5, y_peer[d - 1]))
    for copy in first_b:
        copy.wait_recv()
    total = gram[b_block(y), :].astype(F32)
    for d in range(3):
        total = total + rb1[d].astype(F32)
    sb2[...] = total.astype(BF16)
    for d in (2, 1, 3):
        to = (x + d) % 4
        part = pl.ds(pl.multiple_of(to // 2 * 48, 48), 48)
        cols = pl.ds(pl.multiple_of(to % 2 * 384, 384), 384)
        second.append(send(sb2.at[part, cols], rb2.at[d - 1], rsend, rrecv, d + 8, x_peer[d - 1]))
    for copy in second:
        copy.wait_recv()
    total = sa2[pl.ds(pl.multiple_of(y * 48, 48), 48), :].astype(F32)
    for d in range(3):
        total = total + ra2[d].astype(F32)
    sa3[0, 0:48] = total
    sa3[1, 0:48] = pltpu.roll(total, 192, 1)
    total = sb2[pl.ds(pl.multiple_of(xh * 48, 48), 48), pl.ds(pl.multiple_of(xl * 384, 384), 384)].astype(F32)
    for d in range(3):
        total = total + rb2[d].astype(F32)
    sb3[0, 0:48] = total
    sb3[1, 0:48] = pltpu.roll(total, 192, 1)

    for to in range(8):
        source = sa3 if to < 4 else sb3
        for half in range(2):
            st3[to, half] = source[half, pl.ds(to % 4 * 12, 16), 0:256].astype(BF16)
    third = []
    for d in (4, 3, 5, 2, 6, 1, 7, 0):
        for r in range(2):
            if d or r:
                to = (z + d) % 8
                half = core if r == 0 else 1 - core
                third.append(send(st3.at[to, half], r3.at[d, r], fsend, frecv, d * 2 + r, z_peer[d][r]))
    for copy in third:
        copy.wait_recv()
    total = st3[z, core].astype(F32)
    for d in range(1, 8):
        total = total + r3[d, 0].astype(F32)
    out_ref[core] = total[0:12, 0:192]
    total = r3[0, 1].astype(F32)
    for d in range(1, 8):
        total = total + r3[d, 1].astype(F32)
    out_ref[1 - core] = total[0:12, 0:192]

    for copy in shifts + theirs + [beside] + passed + gathers + first_a + first_b + second + third:
        copy.wait_send()


def per_device(occupied, empty, occ_energy, emp_energy, partner, gvecs):
    waves = jnp.swapaxes(gvecs, 1, 2)
    waves = jnp.concatenate([waves, waves], axis=2)
    order = jnp.broadcast_to(jnp.asarray(row_order()), (2, 1, COLS))
    waves = jnp.concatenate([waves, order, jnp.zeros((2, 4, COLS), jnp.int32)], axis=1)
    vmem = pl.BlockSpec(memory_space=pltpu.VMEM)
    hbm = pl.BlockSpec(memory_space=pl.ANY)
    smem = pl.BlockSpec(memory_space=pltpu.SMEM)
    dma = pltpu.SemaphoreType.DMA
    return pl.pallas_call(
        kernel,
        out_shape=jax.ShapeDtypeStruct((2, 12, 192), F32),
        in_specs=[hbm, hbm, vmem, vmem, smem, vmem, vmem],
        out_specs=vmem,
        scratch_shapes=[
            pltpu.VMEM((3, NO, PTS), BF16),
            pltpu.VMEM((NO, 128), F32),
            pltpu.VMEM((3, NO, 128), F32),
            pltpu.VMEM((4, NB, PTS), BF16),
            pltpu.VMEM((2, NO, PTS), BF16),
            pltpu.VMEM((4, NO, PTS), BF16),
            pltpu.VMEM((4, NX * 128, COLS), BF16),
            pltpu.VMEM((4 * NX, COLS), F32),
            pltpu.VMEM((4 * NX, COLS), F32),
            pltpu.VMEM((NO * NB, NX * 128), BF16),
            pltpu.VMEM((NO * NB, COLS), F32),
            pltpu.VMEM((COLS, COLS), BF16),
            pltpu.VMEM((3, 192, 384), BF16),
            pltpu.VMEM((3, 96, COLS), BF16),
            pltpu.VMEM((192, 384), BF16),
            pltpu.VMEM((96, COLS), BF16),
            pltpu.VMEM((3, 48, 384), BF16),
            pltpu.VMEM((3, 48, 384), BF16),
            pltpu.VMEM((2, 64, 384), F32),
            pltpu.VMEM((2, 64, 384), F32),
            pltpu.VMEM((8, 2, 16, 256), BF16),
            pltpu.VMEM((8, 2, 16, 256), BF16),
            dma((6,)), dma((6,)), dma((8,)), dma((8,)), dma((12,)), dma((12,)), dma((16,)), dma((16,)), dma,
        ],
        compiler_params=pltpu.CompilerParams(
            collective_id=0, has_side_effects=True, vmem_limit_bytes=48 * 1024 * 1024
        ),
    )(occupied, empty, occ_energy, emp_energy, partner, waves, jnp.asarray(yz_table()).astype(BF16))


def solution(mesh):
    placed = (P("ka", None, "row"), P("ka", None, "row"), P("ka", None), P("ka", None), P(), P())
    return jax.shard_map(
        per_device, mesh=mesh, in_specs=placed, out_specs=P(None, "ka", "row"), check_vma=False
    )
```

time: 247 us -> 53.8 us (0.22); the launches traced: 243 us -> 53.6 us
  other arithmetic: 63 us -> 0.07 us
  waiting for transfers between devices: 61.3 us -> 0 us
  Pallas kernels: 0 us -> 49.5 us
  blocking collectives: 46.4 us -> 0 us
  starting transfers between devices: 42.9 us -> 0 us
  matrix products: 16.6 us -> 0 us
  between operations: 4.99 us -> 0.05 us
  local copies, waits for them, and re-layouts: 8.1 us -> 3.96 us
    another operation x1 -> x0, other arithmetic: 54.2 us -> none
    all_to_all x4 -> x0, waiting for transfers between devices: 53.5 us -> none  [the longest x2 27.8 us: summed_on_arrival(): lax.all_to_all(blocks, axis, split_axis=0, concat_axis=0, tiled=True)]
    pallas_call x0 -> x1, Pallas kernels: none -> 49.5 us  [per_device(): pl.pallas_call(kernel, out_shape=jax.ShapeDtypeStruct((2, 12, 192), F32),...]
    all_to_all x1 -> x0, blocking collectives: 46.4 us -> none  [summed_on_arrival(): lax.all_to_all(blocks, axis, split_axis=0, concat_axis=0, tiled=True)]
    all_to_all x4 -> x0, starting transfers between devices: 22.5 us -> none  [the longest x2 13.8 us: summed_on_arrival(): lax.all_to_all(blocks, axis, split_axis=0, concat_axis=0, tiled=True)]
    ppermute x8 -> x0, starting transfers between devices: 20.4 us -> none  [from_behind(): return lax.ppermute(block, axis, route)]
    dot_general x4 -> x0, matrix products: 16.6 us -> none  [the longest x2 13.3 us: per_device(): lax.dot_general(density, table_q, (((1,), (1,)), ((), ())), preferred_ele...]
    ppermute x8 -> x0, waiting for transfers between devices: 7.8 us -> none  [from_behind(): return lax.ppermute(block, axis, route)]
  transfers between devices with their start and end apart: 12 -> 0, of which waited for: 8 -> 0; matrix products, arithmetic and copies ran while one was open for 6% -> 0% of each run, Pallas kernels for 0% -> 0%
where the time goes in v1:
time: 53.8 us; the launch traced here: 53.6 us
  Pallas kernels  49.5 us (92%)
  local copies, waits for them, and re-layouts  3.96 us (7%)
    pallas_call x1, Pallas kernels, per_device(): pl.pallas_call(kernel, out_shape=jax.ShapeDtypeStruct((2, 12, 192), F32),...  49.5 us
    unnamed x15, local copies, waits for them, and re-layouts  3.25 us

profile of v1, /device:TPU:1, one launch (start us, length us, event | category | flops | bytes accessed | tf_op | source)
XLA Modules:
  0.0 53.6 jit_solution(20396619717038985)
XLA Ops:
  0.0 0.0 copy-start.6
  0.0 0.0 copy-start.2
  0.0 0.1 pad.3.clone
  0.1 0.7 %copy.12 = s32[2,384,3]{1,2,0:T(4,128)S(1)} copy(s32[2,384,3]{1,0,2:T(2,128)} %param.13) | data formatting | bytes 18432 | tf_op args[5]
  0.8 0.0 copy-done.6
  0.8 0.0 copy-start.3
  0.8 0.0 copy-start.4
  0.8 0.0 copy-start.5
  0.8 0.1 add_add_fusion.wave_ref
  0.9 0.0 copy-done.2
  0.9 0.6 %copy-done.3 = s32[2,64]{1,0:T(2,128)S(1)} copy-done((s32[2,64]{1,0:T(2,128)S(1)}, s32[2,64]{1,0:T(2,128)}, u32[]{:S(2)}) %copy-start.3) | copy-done | bytes 536
  1.5 0.0 copy-done.4
  1.5 0.0 copy-done.5
  1.5 0.0 copy-start
  1.5 1.0 %copy-done = bf16[1,64,4096]{2,1,0:T(8,128)(2,1)S(1)} copy-done((bf16[1,64,4096]{2,1,0:T(8,128)(2,1)S(1)}, bf16[1,64,4096]{2,1,0:T(8,128)(2,1)}, u32[]{:S(2)}) %copy-start) | copy-done | bytes 524312
  2.5 0.0 copy-start.1
  2.5 0.9 %copy-done.1 = bf16[512,128]{1,0:T(8,128)(2,1)S(1)} copy-done((bf16[512,128]{1,0:T(8,128)(2,1)S(1)}, bf16[512,128]{1,0:T(8,128)(2,1)}, u32[]{:S(2)}) %copy-start.1) | copy-done | bytes 131096
  3.4 49.5 %shard_map.82 = f32[2,12,192]{2,1,0:T(8,128)S(1)} custom-call(bf16[1,8,4096]{2,1,0:T(8,128)(2,1)S(1)} %copy-done.2, bf16[1,64,4096]{2,1,0:T(8,128)(2,1)S(1)} %copy-done, bf16[1,8]{1,0:T(2,128)(2,1)S(1)} %copy-done.4, bf16[1,64]{1,0:T(2,128)(2,1)S(1)} %copy-done.5, s32[2,64]{1,0:T(2,128)S(1)} %copy-done.3, s32[2,8,768]{2,1,0:T(8,128)S(1)} %add_add_fusion.wave_ref, ...), custom_call_target="tpu_custom_call" | custom-call | tf_op jit(solution)/shard_map/pallas_call | solution.py:261
  53.0 0.6 %copy.10 = f32[2,12,192]{2,0,1:T(2,128)} copy(f32[2,12,192]{2,1,0:T(8,128)S(1)} %shard_map.82) | data formatting | bytes 36864 | tf_op jit(solution)/shard_map/pallas_call | solution.py:261
  (2 shorter events, 0.0 us)
Async XLA Ops:
  0.0 0.8 %copy-start.6 = (s32[768]{0:T(1024)S(1)}, s32[768]{0:T(1024)}, u32[]{:S(2)}) copy-start(s32[768]{0:T(1024)} %constant.6.clone) | copy-start | bytes 9220
  0.0 0.9 %copy-start.2 = (bf16[1,8,4096]{2,1,0:T(8,128)(2,1)S(1)}, bf16[1,8,4096]{2,1,0:T(8,128)(2,1)}, u32[]{:S(2)}) copy-start(bf16[1,8,4096]{2,1,0:T(8,128)(2,1)} %occ_ref.1) | copy-start | bytes 196612
  0.8 0.7 %copy-start.3 = (s32[2,64]{1,0:T(2,128)S(1)}, s32[2,64]{1,0:T(2,128)}, u32[]{:S(2)}) copy-start(s32[2,64]{1,0:T(2,128)} %partner_ref.1) | copy-start | bytes 1540
  0.8 0.7 %copy-start.4 = (bf16[1,8]{1,0:T(2,128)(2,1)S(1)}, bf16[1,8]{1,0:T(2,128)(2,1)}, u32[]{:S(2)}) copy-start(bf16[1,8]{1,0:T(2,128)(2,1)} %oe_ref.1) | copy-start | bytes 52
  0.8 0.7 %copy-start.5 = (bf16[1,64]{1,0:T(2,128)(2,1)S(1)}, bf16[1,64]{1,0:T(2,128)(2,1)}, u32[]{:S(2)}) copy-start(bf16[1,64]{1,0:T(2,128)(2,1)} %ee_ref.1) | copy-start | bytes 388
  1.5 1.0 %copy-start = (bf16[1,64,4096]{2,1,0:T(8,128)(2,1)S(1)}, bf16[1,64,4096]{2,1,0:T(8,128)(2,1)}, u32[]{:S(2)}) copy-start(bf16[1,64,4096]{2,1,0:T(8,128)(2,1)} %emp_ref.1) | copy-start | bytes 1572868
  2.5 0.9 %copy-start.1 = (bf16[512,128]{1,0:T(8,128)(2,1)S(1)}, bf16[512,128]{1,0:T(8,128)(2,1)}, u32[]{:S(2)}) copy-start(bf16[512,128]{1,0:T(8,128)(2,1)} %constant.12.yz_ref) | copy-start | bytes 393220

commit v2 on v0

v2 whole, which is shorter than its diff:
```python
import math

import jax
import jax.numpy as jnp
import numpy as np
from jax import lax
from jax.experimental import pallas as pl
from jax.experimental.pallas import tpu as pltpu
from jax.sharding import PartitionSpec as P

MESH = pl.DeviceIdType.MESH
F32 = jnp.float32
BF16 = jnp.bfloat16
NO = 8
NB = 32
NG = 384
PTS = 4096
HALF = PTS // 2
YZ = 512
GZ = 32
COLS = 2 * NG
PAIRS = NO * NB
WIDE = (256, 128)
START = (0, 512)
BLOCKS = (0, 1, 3, 4, 6, 7, 9, 10, 2, 5, 8, 11)
PIECES = ((0, 0), (0, 1), (1, 0), (1, 1), (2, 0), (3, 0), (2, 1), (3, 1))
DIST = (2, 1, 3)


def yz_table():
    point = np.arange(YZ)
    y, z = point // GZ, point % GZ
    table = np.zeros((YZ, 128), np.float64)
    for g1 in range(-4, 5):
        for g2 in range(5):
            turn = 2 * math.pi * ((g1 * y * 2 + g2 * z) % 32) / 32
            column = (g1 + 4) * 5 + g2
            table[:, column] = np.cos(turn)
            table[:, 64 + column] = np.sin(turn)
    return table.astype(np.float32)


def row_order():
    a = np.concatenate([np.arange(64) + 64 * block for block in BLOCKS])
    z, xh, y, i = a // 96, a // 48 % 2, a // 12 % 4, a % 12
    first = xh * 192 + y * 48 + (z % 4) * 12 + i
    second = 384 + y * 96 + xh * 48 + (z % 4) * 12 + i
    return np.where(z < 4, first, second).astype(np.int32).reshape(1, COLS)


def kernel(
    occ_hbm, emp_hbm, oe_ref, ee_ref, partner_ref, wave_ref, order_ref, yz_hbm, out_ref,
    shift0, shift1, oe_src, oe_shift, efull, osel, ofull, yz, wtab, utab, vtab, ybuf, proj, ordering, left_t, right,
    ga0, ga1, gb0, gb1, ra0, ra1, rb0, rb1, ta0, ta1, tb0, tb1, sa0, sa1, sb0, sb1,
    qa0, qa1, qb0, qb1, fa0, fa1, fb0, fb1, st0, st1, r30, r31,
    zsend, zrecv, gsend, grecv, rsend, rrecv, fsend, frecv, lsem,
):
    shift = (shift0, shift1)
    ga, gb, ra, rb = (ga0, ga1), (gb0, gb1), (ra0, ra1), (rb0, rb1)
    ta, tb, sa, sb = (ta0, ta1), (tb0, tb1), (sa0, sa1), (sb0, sb1)
    qa, qb, fa, fb = (qa0, qa1), (qb0, qb1), (fa0, fa1), (fb0, fb1)
    ka, row = lax.axis_index("ka"), lax.axis_index("row")
    z, xh, y = ka // 8, ka // 4 % 2, ka % 4
    xl, core = row // 2, row % 2
    x = xh * 2 + xl

    def device(z_, x_, y_, core_):
        return (z_ * 8 + (x_ // 2) * 4 + y_, (x_ % 2) * 2 + core_)

    sibling = (ka, xl * 2 + 1 - core)
    across = (ka, (1 - xl) * 2 + core)
    diagonal = (ka, (1 - xl) * 2 + 1 - core)
    x_peer = [device(z, (x + d) % 4, y, core) for d in range(1, 4)]
    y_peer = [device(z, x, (y + d) % 4, core) for d in range(1, 4)]
    z_peer = [[device((z + d) % 8, x, y, core if r == 0 else 1 - core) for r in range(2)] for d in range(8)]

    barrier = pltpu.get_barrier_semaphore()
    peers = [sibling, diagonal] + x_peer + y_peer + [z_peer[d][r] for d in range(1, 8) for r in range(2)]
    for peer in peers:
        pl.semaphore_signal(barrier, inc=1, device_id=peer, device_id_type=MESH)

    locals_ = [pltpu.make_async_copy(yz_hbm, yz, lsem.at[0])]
    own_bands = pl.ds(pl.multiple_of(xl * NB, NB), NB)
    their_bands = pl.ds(pl.multiple_of((1 - xl) * NB, NB), NB)
    points = [pl.ds(half * HALF, HALF) for half in range(2)]
    for half in range(2):
        locals_.append(pltpu.make_async_copy(emp_hbm.at[0, own_bands, points[half]], efull.at[0, half], lsem.at[1 + half]))
    for copy in locals_:
        copy.start()

    eye = lax.broadcasted_iota(jnp.int32, (NO, NO), 0) == lax.broadcasted_iota(jnp.int32, (NO, NO), 1)
    levels = jnp.broadcast_to(oe_ref[...].astype(F32), (NO, NO))
    column = jnp.sum(jnp.where(eye, levels, 0.0), axis=1, keepdims=True)
    oe_src[...] = jnp.broadcast_to(column, (NO, 128))
    pl.semaphore_wait(barrier, len(peers))

    sent = []

    def send(src, dst, sends, recvs, index, peer):
        copy = pltpu.make_async_remote_copy(
            src_ref=src, dst_ref=dst, send_sem=sends.at[index], recv_sem=recvs.at[index],
            device_id=peer, device_id_type=MESH,
        )
        copy.start()
        sent.append(copy)
        return copy

    shifts, theirs, beside = [[], []], [], []
    for half in range(2):
        for s in (2, 1, 3):
            shifts[half].append(
                send(occ_hbm.at[0, :, points[half]], shift[half].at[s - 1], zsend, zrecv, half * 3 + s - 1, z_peer[2 * s][0])
            )
        theirs.append(send(emp_hbm.at[0, their_bands, points[half]], efull.at[2, half], gsend, grecv, half, across))
    for s in range(1, 4):
        shifts[1].append(send(oe_src, oe_shift.at[s - 1], zsend, zrecv, 5 + s, z_peer[2 * s][0]))
    for half in range(2):
        beside.append(send(emp_hbm.at[0, own_bands, points[half]], efull.at[1, half], gsend, grecv, 2 + half, sibling))

    def kept(line):
        both = jnp.concatenate([line, line], axis=1)
        return jnp.concatenate([both[:, 64 * block : 64 * block + 64] for block in BLOCKS], axis=1)

    g0, g1, g2 = [
        kept(jnp.where(core == 0, wave_ref[axis, 0:1, :], wave_ref[axis, 1:2, :])) for axis in range(3)
    ]
    flip = jnp.where(g2 < 0, -1, 1)
    group = (flip * g1 + 4) * 5 + flip * g2
    index = lax.broadcasted_iota(jnp.int32, (32, COLS), 0)
    piece = index >> 2
    slot = jnp.where(piece < 4, piece >> 1, 2 + (piece & 1))
    half_of = jnp.where(piece < 4, piece & 1, (piece - 4) >> 1)
    src_core = (core + slot) & 1
    src_xl = (xl + (slot >> 1)) & 1
    plane = (src_xl * 2 + src_core) * 8 + half_of * 4 + (index & 3)
    lane = lax.broadcasted_iota(jnp.int32, (32, COLS), 1)
    is_cos = (lane < 256) | ((lane >= 512) & (lane < 640))
    quarter = jnp.where(is_cos, 0, 8)
    turn = ((g0 * plane - quarter) & 31).astype(F32) * (2.0 * math.pi / 32)
    utab[...] = jnp.cos(turn)
    vtab[...] = jnp.sin(turn) * (-flip).astype(F32)
    chosen = lax.broadcasted_iota(jnp.int32, (64, COLS), 0) == group

    def fill(i, carry):
        u = utab[pl.ds(i, 1), :]
        v = vtab[pl.ds(i, 1), :]
        base = pl.multiple_of(i * 128, 128)
        wtab[pl.ds(base, 64), :] = jnp.where(chosen, u, 0.0).astype(BF16)
        wtab[pl.ds(base + 64, 64), :] = jnp.where(chosen, v, 0.0).astype(BF16)
        return carry

    lax.fori_loop(0, 16, fill, 0)

    steps = [jnp.clip(partner_ref[q, 0] // 16, 1, 3) - 1 for q in range(2)]
    passed, gathers = [], [[], []]

    def pass_on(half):
        theirs[half].wait_recv()
        passed.append(send(efull.at[2, half], efull.at[3, half], gsend, grecv, 4 + half, sibling))

    def select(half):
        for copy in shifts[half]:
            copy.wait_recv()
        for q in range(2):
            osel[half, q] = shift[half][steps[q]]
        gathers[half].append(send(osel.at[half, 1 - core], ofull.at[1, half], gsend, grecv, 6 + half, sibling))
        gathers[half].append(send(osel.at[half, core], ofull.at[2, half], gsend, grecv, 8 + half, across))
        gathers[half].append(send(osel.at[half, 1 - core], ofull.at[3, half], gsend, grecv, 10 + half, diagonal))
        ofull[0, half] = osel[half, core]

    def project(number):
        slot, half = PIECES[number]
        for i in range(4):
            lanes = slice(i * YZ, (i + 1) * YZ)
            e = efull[slot, half, :, lanes].astype(F32)
            o = ofull[slot, half, :, lanes].astype(F32)
            density = jnp.concatenate([(o[v : v + 1] * e).astype(BF16) for v in range(NO)], axis=0)
            part = jnp.dot(density, yz[...], preferred_element_type=F32)
            first = (number * 4 + i) * 128
            ybuf[:, first : first + 128] = part.astype(BF16)

    def gathered(begin, end):
        return jnp.dot(ybuf[:, begin * 512 : end * 512], wtab[begin * 512 : end * 512, :], preferred_element_type=F32)

    pass_on(0)
    select(0)
    lax.fori_loop(16, 32, fill, 0)
    ordering[...] = jnp.where(
        lax.broadcasted_iota(jnp.int32, (COLS, COLS), 0) == order_ref[...], 1.0, 0.0
    ).astype(BF16)
    for copy in locals_:
        copy.wait()
    project(0)
    pass_on(1)
    select(1)

    oe = jnp.where(core == 0, oe_shift[steps[0]], oe_shift[steps[1]])
    pick = lax.broadcasted_iota(jnp.int32, (NB, 2 * NB), 1) == lax.broadcasted_iota(jnp.int32, (NB, 2 * NB), 0) + xl * NB
    ee = jnp.broadcast_to(ee_ref[...].astype(F32), (NB, 2 * NB))
    ee = jnp.sum(jnp.where(pick, ee, 0.0), axis=1, keepdims=True)
    weight = jnp.concatenate([1.0 / (ee - oe[v : v + 1, 0:1]) for v in range(NO)], axis=0)

    project(1)
    for half in range(2):
        beside[half].wait_recv()
        gathers[half][0].wait_recv()
        project(2 + half)
    proj[...] = gathered(0, 4)
    for half in range(2):
        gathers[half][1].wait_recv()
        project(4 + 2 * half)
        gathers[half][2].wait_recv()
        passed[half].wait_recv()
        project(5 + 2 * half)
        if half == 0:
            proj[...] = proj[...] + gathered(4, 6)

    value = (proj[...] + gathered(6, 8)) * (1.0 / (4 * PTS))
    left = value.astype(BF16)
    right[...] = (weight * value).astype(BF16)
    left_t[...] = lax.dot_general(
        ordering[...], left, (((1,), (1,)), ((), ())), preferred_element_type=F32
    ).astype(BF16)

    def a_block(h, x_):
        cols = pl.ds(pl.multiple_of(START[h] + x_ % 2 * WIDE[h], WIDE[h]), WIDE[h])
        return jnp.dot(left_t[pl.ds(pl.multiple_of(x_ // 2 * 192, 192), 192), :], right[:, cols], preferred_element_type=F32)

    def b_block(h, y_):
        rows = pl.ds(pl.multiple_of(384 + y_ * 96, 96), 96)
        return jnp.dot(left_t[rows, :], right[:, START[h] : START[h] + 2 * WIDE[h]], preferred_element_type=F32)

    first_a, first_b, second = [[], []], [[], []], [[], []]
    for h in range(2):
        for d in DIST:
            ga[h][d - 1] = a_block(h, (x + d) % 4).astype(BF16)
            first_a[h].append(send(ga[h].at[d - 1], ra[h].at[d - 1], rsend, rrecv, h * 12 + d - 1, x_peer[d - 1]))
            gb[h][d - 1] = b_block(h, (y + d) % 4).astype(BF16)
            first_b[h].append(send(gb[h].at[d - 1], rb[h].at[d - 1], rsend, rrecv, h * 12 + d + 2, y_peer[d - 1]))
    for h in range(2):
        ta[h][...] = a_block(h, x)
        tb[h][...] = b_block(h, y)

    def sum_first(h):
        for copy in first_a[h]:
            copy.wait_recv()
        total = ta[h][...]
        for d in range(3):
            total = total + ra[h][d].astype(F32)
        ta[h][...] = total
        sa[h][...] = total.astype(BF16)
        for d in DIST:
            rows = pl.ds(pl.multiple_of((y + d) % 4 * 48, 48), 48)
            second[h].append(send(sa[h].at[rows], qa[h].at[d - 1], rsend, rrecv, h * 12 + d + 5, y_peer[d - 1]))
        for copy in first_b[h]:
            copy.wait_recv()
        total = tb[h][...]
        for d in range(3):
            total = total + rb[h][d].astype(F32)
        tb[h][...] = total
        sb[h][...] = total.astype(BF16)
        for d in DIST:
            to = (x + d) % 4
            rows = pl.ds(pl.multiple_of(to // 2 * 48, 48), 48)
            cols = pl.ds(pl.multiple_of(to % 2 * WIDE[h], WIDE[h]), WIDE[h])
            second[h].append(send(sb[h].at[rows, cols], qb[h].at[d - 1], rsend, rrecv, h * 12 + d + 8, x_peer[d - 1]))

    third = [[], []]

    def sum_second(h):
        for copy in second[h]:
            copy.wait_recv()
        total = ta[h][pl.ds(pl.multiple_of(y * 48, 48), 48), :]
        for d in range(3):
            total = total + qa[h][d].astype(F32)
        fa[h][0:48, :] = total
        total = tb[h][pl.ds(pl.multiple_of(xh * 48, 48), 48), pl.ds(pl.multiple_of(xl * WIDE[h], WIDE[h]), WIDE[h])]
        for d in range(3):
            total = total + qb[h][d].astype(F32)
        fb[h][0:48, :] = total
        for to in range(8):
            source = fa[h] if to < 4 else fb[h]
            if h == 0:
                for half in range(2):
                    st0[to, half] = source[to % 4 * 12 : to % 4 * 12 + 16, half * 128 : half * 128 + 128].astype(BF16)
            else:
                st1[to] = source[to % 4 * 12 : to % 4 * 12 + 16, :].astype(BF16)
        for d in (4, 3, 5, 2, 6, 1, 7, 0):
            for r in range(2):
                if d or r:
                    to = (z + d) % 8
                    if h == 0:
                        src, dst = st0.at[to, core if r == 0 else 1 - core], r30.at[d, r]
                    else:
                        src, dst = st1.at[to], r31.at[d, r]
                    third[h].append(send(src, dst, fsend, frecv, h * 16 + d * 2 + r, z_peer[d][r]))

    sum_first(0)
    sum_first(1)
    sum_second(0)
    sum_second(1)

    def sum_third(h):
        for copy in third[h]:
            copy.wait_recv()
        landed = (r30, r31)[h]
        mine = (st0[z, core] if h == 0 else st1[z]).astype(F32)
        other = landed[0, 1].astype(F32)
        for d in range(1, 8):
            mine = mine + landed[d, 0].astype(F32)
            other = other + landed[d, 1].astype(F32)
        first = jnp.where(core == 0, mine, other)[0:12]
        last = jnp.where(core == 0, other, mine)[0:12]
        for q, total in enumerate((first, last)):
            if h == 0:
                out_ref[:, q, 0:128] = total
            else:
                out_ref[:, q, 128:192] = jnp.where(core == 0, total[:, 0:64], total[:, 64:128])

    sum_third(0)
    sum_third(1)
    for copy in sent:
        copy.wait_send()


def per_device(occupied, empty, occ_energy, emp_energy, partner, gvecs):
    waves = jnp.transpose(gvecs, (2, 0, 1))
    vmem = pl.BlockSpec(memory_space=pltpu.VMEM)
    hbm = pl.BlockSpec(memory_space=pl.ANY)
    smem = pl.BlockSpec(memory_space=pltpu.SMEM)
    dma = pltpu.SemaphoreType.DMA

    def chunks(shape, dtype=BF16):
        return [pltpu.VMEM(shape(width), dtype) for width in WIDE]

    out = pl.pallas_call(
        kernel,
        out_shape=jax.ShapeDtypeStruct((12, 2, 192), F32),
        in_specs=[hbm, hbm, vmem, vmem, smem, vmem, vmem, hbm],
        out_specs=vmem,
        scratch_shapes=[
            pltpu.VMEM((3, NO, HALF), BF16),
            pltpu.VMEM((3, NO, HALF), BF16),
            pltpu.VMEM((NO, 128), F32),
            pltpu.VMEM((3, NO, 128), F32),
            pltpu.VMEM((4, 2, NB, HALF), BF16),
            pltpu.VMEM((2, 2, NO, HALF), BF16),
            pltpu.VMEM((4, 2, NO, HALF), BF16),
            pltpu.VMEM((YZ, 128), BF16),
            pltpu.VMEM((4096, COLS), BF16),
            pltpu.VMEM((32, COLS), F32),
            pltpu.VMEM((32, COLS), F32),
            pltpu.VMEM((PAIRS, 4096), BF16),
            pltpu.VMEM((PAIRS, COLS), F32),
            pltpu.VMEM((COLS, COLS), BF16),
            pltpu.VMEM((COLS, PAIRS), BF16),
            pltpu.VMEM((PAIRS, COLS), BF16),
        ]
        + chunks(lambda width: (3, 192, width))
        + chunks(lambda width: (3, 96, 2 * width))
        + chunks(lambda width: (3, 192, width))
        + chunks(lambda width: (3, 96, 2 * width))
        + chunks(lambda width: (192, width), F32)
        + chunks(lambda width: (96, 2 * width), F32)
        + chunks(lambda width: (192, width))
        + chunks(lambda width: (96, 2 * width))
        + chunks(lambda width: (3, 48, width))
        + chunks(lambda width: (3, 48, width))
        + chunks(lambda width: (64, width), F32)
        + chunks(lambda width: (64, width), F32)
        + [
            pltpu.VMEM((8, 2, 16, 128), BF16),
            pltpu.VMEM((8, 16, 128), BF16),
            pltpu.VMEM((8, 2, 16, 128), BF16),
            pltpu.VMEM((8, 2, 16, 128), BF16),
            dma((9,)), dma((9,)), dma((12,)), dma((12,)), dma((24,)), dma((24,)), dma((32,)), dma((32,)), dma((3,)),
        ],
        compiler_params=pltpu.CompilerParams(
            collective_id=0, has_side_effects=True, vmem_limit_bytes=60 * 1024 * 1024
        ),
    )(
        occupied, empty, occ_energy, emp_energy, partner, waves,
        jnp.asarray(row_order()), jnp.asarray(yz_table()).astype(BF16),
    )
    return jnp.swapaxes(out, 0, 1)


def solution(mesh):
    placed = (P("ka", None, "row"), P("ka", None, "row"), P("ka", None), P("ka", None), P(), P())
    return jax.shard_map(
        per_device, mesh=mesh, in_specs=placed, out_specs=P(None, "ka", "row"), check_vma=False
    )
```

time: 247 us -> 49.8 us (0.20); the launches traced: 243 us -> 49.6 us
  other arithmetic: 63 us -> 0 us
  waiting for transfers between devices: 61.3 us -> 0 us
  Pallas kernels: 0 us -> 48.3 us
  blocking collectives: 46.4 us -> 0 us
  starting transfers between devices: 42.9 us -> 0 us
  matrix products: 16.6 us -> 0 us
  local copies, waits for them, and re-layouts: 8.1 us -> 1.35 us
  between operations: 4.99 us -> 0.01 us
    another operation x1 -> x0, other arithmetic: 54.2 us -> none
    all_to_all x4 -> x0, waiting for transfers between devices: 53.5 us -> none  [the longest x2 27.8 us: summed_on_arrival(): lax.all_to_all(blocks, axis, split_axis=0, concat_axis=0, tiled=True)]
    pallas_call x0 -> x1, Pallas kernels: none -> 48.3 us  [per_device(): pl.pallas_call(kernel, out_shape=jax.ShapeDtypeStruct((12, 2, 192), F32),...]
    all_to_all x1 -> x0, blocking collectives: 46.4 us -> none  [summed_on_arrival(): lax.all_to_all(blocks, axis, split_axis=0, concat_axis=0, tiled=True)]
    all_to_all x4 -> x0, starting transfers between devices: 22.5 us -> none  [the longest x2 13.8 us: summed_on_arrival(): lax.all_to_all(blocks, axis, split_axis=0, concat_axis=0, tiled=True)]
    ppermute x8 -> x0, starting transfers between devices: 20.4 us -> none  [from_behind(): return lax.ppermute(block, axis, route)]
    dot_general x4 -> x0, matrix products: 16.6 us -> none  [the longest x2 13.3 us: per_device(): lax.dot_general(density, table_q, (((1,), (1,)), ((), ())), preferred_ele...]
    ppermute x8 -> x0, waiting for transfers between devices: 7.8 us -> none  [from_behind(): return lax.ppermute(block, axis, route)]
  transfers between devices with their start and end apart: 12 -> 0, of which waited for: 8 -> 0; matrix products, arithmetic and copies ran while one was open for 6% -> 0% of each run, Pallas kernels for 0% -> 0%
where the time goes in v2:
time: 49.8 us; the launch traced here: 49.6 us
  Pallas kernels  48.3 us (97%)
  local copies, waits for them, and re-layouts  1.35 us (3%)
    pallas_call x1, Pallas kernels, per_device(): pl.pallas_call(kernel, out_shape=jax.ShapeDtypeStruct((12, 2, 192), F32),...  48.3 us
    unnamed x1, local copies, waits for them, and re-layouts  1.35 us

profile of v2, /device:TPU:1, one launch (start us, length us, event | category | flops | bytes accessed | tf_op | source)
XLA Modules:
  0.0 49.6 jit_solution(17331977570775617308)
XLA Ops:
  0.0 48.3 %shard_map.82 = f32[12,2,192]{2,1,0:T(2,128)} custom-call(bf16[1,8,4096]{2,1,0:T(8,128)(2,1)} %occ_hbm.1, bf16[1,64,4096]{2,1,0:T(8,128)(2,1)} %emp_hbm.1, bf16[1,8]{1,0:T(2,128)(2,1)} %oe_ref.1, bf16[1,64]{1,0:T(2,128)(2,1)} %ee_ref.1, s32[2,64]{1,0:T(2,128)} %partner_ref.1, s32[3,2,384]{2,1,0:T(2,128)} %bitcast.3, s32[1,768]{1,0:T(1,128)} %constant.4.clone.order_ref, ...), custom_call_target="tpu_custom_call" | custom-call | tf_op jit(solution)/shard_map/pallas_call | solution.py:336
  48.3 1.3 %copy.10 = f32[2,12,192]{2,0,1:T(2,128)} copy(f32[2,12,192]{2,0,1:T(2,128)} %bitcast.2) | data formatting | bytes 36864

commit v3 on v0

v3 whole, which is shorter than its diff:
```python
import math

import jax
import jax.numpy as jnp
import numpy as np
from jax import lax
from jax.experimental import pallas as pl
from jax.experimental.pallas import tpu as pltpu
from jax.sharding import PartitionSpec as P

MESH = pl.DeviceIdType.MESH
F32 = jnp.float32
BF16 = jnp.bfloat16
NO = 8
NE = 64
NG = 384
PTS = 4096
HALF = PTS // 2
QUART = PTS // 4
YZ = 512
GZ = 32
COLS = 2 * NG
OWN = COLS // 2
PAIRS = NO * NE
BLOCKS = (0, 1, 6, 7, 2, 8, 3, 4, 9, 10, 5, 11)
PIECES = tuple((slot, part) for slot in range(2) for part in range(4)) + tuple(
    (slot, part) for part in range(4) for slot in (2, 3)
)


def yz_table():
    point = np.arange(YZ)
    y, z = point // GZ, point % GZ
    table = np.zeros((YZ, 128), np.float64)
    for g1 in range(-4, 5):
        for g2 in range(5):
            turn = 2 * math.pi * ((g1 * y * 2 + g2 * z) % 32) / 32
            column = (g1 + 4) * 5 + g2
            table[:, column] = np.cos(turn)
            table[:, 64 + column] = np.sin(turn)
    return table.astype(np.float32)


def row_order():
    a = np.concatenate([np.arange(64) + 64 * block for block in BLOCKS])
    z, xh, y, i = a // 96, a // 48 % 2, a // 12 % 4, a % 12
    first = y * 96 + xh * 48 + (z % 4) * 12 + i
    second = 384 + xh * 192 + y * 48 + (z % 4) * 12 + i
    return np.where(z < 4, first, second).astype(np.int32).reshape(1, COLS)


def kernel(
    occ_hbm, emp_hbm, oe_hbm, ee_hbm, partner_hbm, wave_hbm, order_hbm, yz_hbm, out_ref,
    oe_ref, ee_ref, partner_ref, wave_ref, order_ref,
    shift0, shift1, oe_src, oe_shift, efull, osel, ofull, yz, wtab, utab, vtab, ybuf, proj, ordering, left_t, right,
    ga, gb, ra, rb, ta, tb, sa, sb, qa, qb, fa, fb, st, r3,
    zsend, zrecv, gsend, grecv, rsend, rrecv, fsend, frecv, lsem,
):
    shift = (shift0, shift1)
    ka, row = lax.axis_index("ka"), lax.axis_index("row")
    z, xh, y = ka // 8, ka // 4 % 2, ka % 4
    xl, core = row // 2, row % 2

    def device(z_, xh_, y_, xl_, core_):
        return (z_ * 8 + xh_ * 4 + y_, xl_ * 2 + core_)

    sibling = device(z, xh, y, xl, 1 - core)
    beyond = device(z, 1 - xh, y, xl, core)
    y_peer = [device(z, xh, (y + d) % 4, xl, core) for d in range(1, 4)]
    z_peer = [[device((z + d) % 8, xh, y, xl if r == 0 else 1 - xl, core) for r in range(2)] for d in range(8)]
    across = z_peer[0][1]

    barrier = pltpu.get_barrier_semaphore()
    peers = [z_peer[d][r] for d in (4, 3, 5, 2, 6, 1, 7) for r in range(2)] + [beyond] + y_peer + [across, sibling]
    for peer in peers:
        pl.semaphore_signal(barrier, inc=1, device_id=peer, device_id_type=MESH)

    small = []
    for number, (src, dst) in enumerate(
        [(oe_hbm, oe_ref), (wave_hbm, wave_ref), (ee_hbm, ee_ref), (partner_hbm, partner_ref), (order_hbm, order_ref), (yz_hbm, yz)]
    ):
        small.append(pltpu.make_async_copy(src, dst, lsem.at[number]))
    local = []
    points = [pl.ds(part * QUART, QUART) for part in range(4)]
    for part in range(4):
        local.append(pltpu.make_async_copy(emp_hbm.at[0, :, points[part]], efull.at[0, part], lsem.at[6 + part]))
    for copy in small + local:
        copy.start()
    small[0].wait()

    eye = lax.broadcasted_iota(jnp.int32, (NO, NO), 0) == lax.broadcasted_iota(jnp.int32, (NO, NO), 1)
    levels = jnp.broadcast_to(oe_ref[...].astype(F32), (NO, NO))
    column = jnp.sum(jnp.where(eye, levels, 0.0), axis=1, keepdims=True)
    oe_src[...] = jnp.broadcast_to(column, (NO, 128))
    pl.semaphore_wait(barrier, len(peers))

    sent = []

    def send(src, dst, sends, recvs, index, peer):
        copy = pltpu.make_async_remote_copy(
            src_ref=src, dst_ref=dst, send_sem=sends.at[index], recv_sem=recvs.at[index],
            device_id=peer, device_id_type=MESH,
        )
        copy.start()
        sent.append(copy)
        return copy

    shifts, theirs, beside = [[], []], [], []

    def cross(part):
        theirs.append(send(emp_hbm.at[0, :, points[part]], efull.at[2, part], gsend, grecv, part, across))

    for half in range(2):
        for s in (2, 1, 3):
            src = occ_hbm.at[0, :, pl.ds(half * HALF, HALF)]
            shifts[half].append(send(src, shift[half].at[s - 1], zsend, zrecv, half * 3 + s - 1, z_peer[2 * s][0]))
        cross(half)
    for s in range(1, 4):
        shifts[1].append(send(oe_src, oe_shift.at[s - 1], zsend, zrecv, 5 + s, z_peer[2 * s][0]))
    for part in range(4):
        beside.append(send(emp_hbm.at[0, :, points[part]], efull.at[1, part], gsend, grecv, 4 + part, sibling))

    for copy in small[1:]:
        copy.wait()

    def kept(line):
        both = jnp.concatenate([line, line], axis=1)
        return jnp.concatenate([both[:, 64 * block : 64 * block + 64] for block in BLOCKS], axis=1)

    g0, g1, g2 = [
        kept(jnp.where(xl == 0, wave_ref[axis, 0:1, :], wave_ref[axis, 1:2, :])) for axis in range(3)
    ]
    flip = jnp.where(g2 < 0, -1, 1)
    group = (flip * g1 + 4) * 5 + flip * g2
    index = lax.broadcasted_iota(jnp.int32, (32, COLS), 0)
    late = index - 16
    slot_of = jnp.where(index < 16, index >> 3, 2 + ((late >> 1) & 1))
    plane_of = jnp.where(index < 16, index & 7, (late >> 2) * 2 + (late & 1))
    src_core = (core + slot_of) & 1
    src_xl = (xl + (slot_of >> 1)) & 1
    plane = (src_xl * 2 + src_core) * 8 + plane_of
    lane = lax.broadcasted_iota(jnp.int32, (32, COLS), 1)
    lane = jnp.where(lane < OWN, lane, lane - OWN)
    is_cos = (lane < 128) | ((lane >= 256) & (lane < 320))
    turn = ((g0 * plane - jnp.where(is_cos, 0, 8)) & 31).astype(F32) * (2.0 * math.pi / 32)
    utab[...] = jnp.cos(turn)
    vtab[...] = jnp.sin(turn) * (-flip).astype(F32)
    chosen = lax.broadcasted_iota(jnp.int32, (64, COLS), 0) == group

    def fill(i, carry):
        u = utab[pl.ds(i, 1), :]
        v = vtab[pl.ds(i, 1), :]
        base = pl.multiple_of(i * 128, 128)
        wtab[pl.ds(base, 64), :] = jnp.where(chosen, u, 0.0).astype(BF16)
        wtab[pl.ds(base + 64, 64), :] = jnp.where(chosen, v, 0.0).astype(BF16)
        return carry

    steps = [jnp.clip(partner_ref[q, 0] // 16, 1, 3) - 1 for q in range(2)]
    passed, passed_occ, occ_beside, occ_across = [], [], [], []

    def pass_on(part):
        theirs[part].wait_recv()
        passed.append(send(efull.at[2, part], efull.at[3, part], gsend, grecv, 8 + part, sibling))

    def pass_occ(half):
        occ_across[half].wait_recv()
        passed_occ.append(send(ofull.at[2, half], ofull.at[3, half], gsend, grecv, 16 + half, sibling))

    def select(half):
        for copy in shifts[half]:
            copy.wait_recv()
        for q in range(2):
            osel[half, q] = shift[half][steps[q]]
        occ_across.append(send(osel.at[half, 1 - xl], ofull.at[2, half], gsend, grecv, 14 + half, across))
        occ_beside.append(send(osel.at[half, xl], ofull.at[1, half], gsend, grecv, 12 + half, sibling))
        ofull[0, half] = osel[half, xl]

    def project(number):
        slot, part = PIECES[number]
        for i in range(2):
            first = i * YZ
            e = efull[slot, part, :, first : first + YZ]
            first += part % 2 * QUART
            o = ofull[slot, part // 2, :, first : first + YZ]
            density = jnp.concatenate([o[v : v + 1] * e for v in range(NO)], axis=0)
            term = jnp.dot(density, yz[...], preferred_element_type=F32)
            first = (number * 2 + i) * 128
            ybuf[:, first : first + 128] = term.astype(BF16)

    def gathered(begin, end):
        return jnp.dot(ybuf[:, begin * 256 : end * 256], wtab[begin * 256 : end * 256, :], preferred_element_type=F32)

    lax.fori_loop(0, 16, fill, 0)
    select(0)
    cross(2)
    pass_on(0)
    lax.fori_loop(16, 32, fill, 0)
    select(1)
    cross(3)
    pass_occ(0)
    pass_on(1)
    for part in range(4):
        local[part].wait()
        project(part)
    occ_beside[0].wait_recv()
    occ_beside[1].wait_recv()
    for part in range(4):
        beside[part].wait_recv()
        project(4 + part)
    proj[...] = gathered(0, 8)
    pass_occ(1)
    pass_on(2)
    ordering[...] = jnp.where(
        lax.broadcasted_iota(jnp.int32, (COLS, COLS), 0) == order_ref[...], 1.0, 0.0
    ).astype(BF16)

    oe = jnp.where(xl == 0, oe_shift[steps[0]], oe_shift[steps[1]])
    pick = lax.broadcasted_iota(jnp.int32, (NE, NE), 1) == lax.broadcasted_iota(jnp.int32, (NE, NE), 0)
    ee = jnp.broadcast_to(ee_ref[...].astype(F32), (NE, NE))
    ee = jnp.sum(jnp.where(pick, ee, 0.0), axis=1, keepdims=True)
    weight = jnp.concatenate([1.0 / (ee - oe[v : v + 1, 0:1]) for v in range(NO)], axis=0)

    for part in range(4):
        project(8 + 2 * part)
        passed[part].wait_recv()
        if part % 2 == 0:
            passed_occ[part // 2].wait_recv()
        project(9 + 2 * part)
        if part == 1:
            pass_on(3)
        if part < 3:
            proj[...] = proj[...] + gathered(8 + 2 * part, 10 + 2 * part)
    proj[...] = (proj[...] + gathered(14, 16)) * (1.0 / (4 * PTS))
    left = proj[...].astype(BF16)
    right[...] = (weight * proj[:, pl.ds(pl.multiple_of(core * OWN, OWN), OWN)]).astype(BF16)
    left_t[...] = lax.dot_general(
        ordering[...], left, (((1,), (1,)), ((), ())), preferred_element_type=F32
    ).astype(BF16)

    def a_block(y_):
        rows = pl.ds(pl.multiple_of(y_ * 96, 96), 96)
        return jnp.dot(left_t[rows, :], right[...], preferred_element_type=F32)

    def b_block(xh_):
        rows = pl.ds(pl.multiple_of(384 + xh_ * 192, 192), 192)
        return jnp.dot(left_t[rows, :], right[...], preferred_element_type=F32)

    gb[...] = b_block(1 - xh).astype(BF16)
    first_b = send(gb, rb, rsend, rrecv, 3, beyond)
    first_a, second_b = [], []
    for d in (2, 1, 3):
        ga[d - 1] = a_block((y + d) % 4).astype(BF16)
        first_a.append(send(ga.at[d - 1], ra.at[d - 1], rsend, rrecv, d - 1, y_peer[d - 1]))
    ta[...] = a_block(y)
    tb[...] = b_block(xh)

    for copy in first_a:
        copy.wait_recv()
    total = ta[...]
    for d in range(3):
        total = total + ra[d].astype(F32)
    ta[...] = total
    sa[...] = total.astype(BF16)
    rows = pl.ds(pl.multiple_of((1 - xh) * 48, 48), 48)
    second_a = send(sa.at[rows], qa, rsend, rrecv, 4, beyond)
    first_b.wait_recv()
    total = tb[...] + rb[...].astype(F32)
    tb[...] = total
    sb[...] = total.astype(BF16)
    for d in (2, 1, 3):
        rows = pl.ds(pl.multiple_of((y + d) % 4 * 48, 48), 48)
        second_b.append(send(sb.at[rows], qb.at[d - 1], rsend, rrecv, d + 4, y_peer[d - 1]))

    third = {}

    def ready(source, first):
        for to in range(4):
            rows = slice(to * 12, to * 12 + 16)
            tail = source[rows, 256:384].astype(BF16)
            for side in range(2):
                st[first + to, side, :, 0:128] = source[rows, side * 128 : side * 128 + 128].astype(BF16)
                st[first + to, side, :, 128:256] = tail

    second_a.wait_recv()
    fa[0:48, :] = ta[pl.ds(pl.multiple_of(xh * 48, 48), 48), :] + qa[...].astype(F32)
    ready(fa, 0)
    for copy in second_b:
        copy.wait_recv()
    total = tb[pl.ds(pl.multiple_of(y * 48, 48), 48), :]
    for d in range(3):
        total = total + qb[d].astype(F32)
    fb[0:48, :] = total
    ready(fb, 4)
    for d in (4, 3, 5, 2, 6, 1, 7, 0):
        for r in range(2):
            if d or r:
                side = xl if r == 0 else 1 - xl
                third[d, r] = send(st.at[(z + d) % 8, side], r3.at[d, r], fsend, frecv, d * 2 + r, z_peer[d][r])
    mine = st[z, xl].astype(F32)
    other = jnp.zeros((16, 256), F32)
    for d in (0, 1, 7, 2, 6, 3, 5, 4):
        if d:
            third[d, 0].wait_recv()
            mine = mine + r3[d, 0].astype(F32)
        third[d, 1].wait_recv()
        other = other + r3[d, 1].astype(F32)
    for q in range(2):
        total = jnp.where(xl == q, mine, other)[0:12]
        out_ref[q, :, 0:128] = total[:, 0:128]
        out_ref[q, :, 128:192] = jnp.where(xl == 0, total[:, 128:192], total[:, 192:256])
    for copy in sent:
        copy.wait_send()


def per_device(occupied, empty, occ_energy, emp_energy, partner, gvecs):
    waves = jnp.transpose(gvecs, (2, 0, 1))
    hbm = pl.BlockSpec(memory_space=pl.ANY)
    dma = pltpu.SemaphoreType.DMA
    return pl.pallas_call(
        kernel,
        out_shape=jax.ShapeDtypeStruct((2, 12, 192), F32),
        in_specs=[hbm] * 8,
        out_specs=pl.BlockSpec(memory_space=pltpu.VMEM),
        scratch_shapes=[
            pltpu.VMEM((1, NO), BF16),
            pltpu.VMEM((1, NE), BF16),
            pltpu.SMEM((2, 64), jnp.int32),
            pltpu.VMEM((3, 2, NG), jnp.int32),
            pltpu.VMEM((1, COLS), jnp.int32),
            pltpu.VMEM((3, NO, HALF), BF16),
            pltpu.VMEM((3, NO, HALF), BF16),
            pltpu.VMEM((NO, 128), F32),
            pltpu.VMEM((3, NO, 128), F32),
            pltpu.VMEM((4, 4, NE, QUART), BF16),
            pltpu.VMEM((2, 2, NO, HALF), BF16),
            pltpu.VMEM((4, 2, NO, HALF), BF16),
            pltpu.VMEM((YZ, 128), BF16),
            pltpu.VMEM((4096, COLS), BF16),
            pltpu.VMEM((32, COLS), F32),
            pltpu.VMEM((32, COLS), F32),
            pltpu.VMEM((PAIRS, 4096), BF16),
            pltpu.VMEM((PAIRS, COLS), F32),
            pltpu.VMEM((COLS, COLS), BF16),
            pltpu.VMEM((COLS, PAIRS), BF16),
            pltpu.VMEM((PAIRS, OWN), BF16),
            pltpu.VMEM((3, 96, OWN), BF16),
            pltpu.VMEM((192, OWN), BF16),
            pltpu.VMEM((3, 96, OWN), BF16),
            pltpu.VMEM((192, OWN), BF16),
            pltpu.VMEM((96, OWN), F32),
            pltpu.VMEM((192, OWN), F32),
            pltpu.VMEM((96, OWN), BF16),
            pltpu.VMEM((192, OWN), BF16),
            pltpu.VMEM((48, OWN), BF16),
            pltpu.VMEM((3, 48, OWN), BF16),
            pltpu.VMEM((64, OWN), F32),
            pltpu.VMEM((64, OWN), F32),
            pltpu.VMEM((8, 2, 16, 256), BF16),
            pltpu.VMEM((8, 2, 16, 256), BF16),
            dma((9,)), dma((9,)), dma((18,)), dma((18,)), dma((8,)), dma((8,)), dma((16,)), dma((16,)), dma((10,)),
        ],
        compiler_params=pltpu.CompilerParams(
            collective_id=0, has_side_effects=True, vmem_limit_bytes=60 * 1024 * 1024
        ),
    )(
        occupied, empty, occ_energy, emp_energy, partner, waves,
        jnp.asarray(row_order()), jnp.asarray(yz_table()).astype(BF16),
    )


def solution(mesh):
    placed = (P("ka", None, "row"), P("ka", None, "row"), P("ka", None), P("ka", None), P(), P())
    return jax.shard_map(
        per_device, mesh=mesh, in_specs=placed, out_specs=P(None, "ka", "row"), check_vma=False
    )
```

time: 247 us -> 50.7 us (0.21)
  the two profiles are of different devices: /device:TPU:1 before, /device:TPU:2 now
where the time goes in v3:
time: 50.7 us; the launch traced here: 50.6 us
  Pallas kernels  49.2 us (97%)
  local copies, waits for them, and re-layouts  1.39 us (3%)
    pallas_call x1, Pallas kernels, per_device(): pl.pallas_call(kernel, out_shape=jax.ShapeDtypeStruct((2, 12, 192), F32),...  49.2 us
    pallas_call x1, local copies, waits for them, and re-layouts, per_device(): pl.pallas_call(kernel, out_shape=jax.ShapeDtypeStruct((2, 12, 192), F32),...  1.39 us

profile of v3, /device:TPU:2, one launch (start us, length us, event | category | flops | bytes accessed | tf_op | source)
XLA Modules:
  0.0 50.6 jit_solution(4914840510935641629)
XLA Ops:
  0.0 49.2 %shard_map.82 = f32[2,12,192]{2,1,0:T(8,128)} custom-call(bf16[1,8,4096]{2,1,0:T(8,128)(2,1)} %occ_hbm.1, bf16[1,64,4096]{2,1,0:T(8,128)(2,1)} %emp_hbm.1, bf16[1,8]{1,0:T(2,128)(2,1)} %oe_hbm.1, bf16[1,64]{1,0:T(2,128)(2,1)} %ee_hbm.1, s32[2,64]{1,0:T(2,128)} %partner_hbm.1, s32[3,2,384]{2,1,0:T(2,128)} %bitcast.1, s32[1,768]{1,0:T(1,128)} %constant.4.clone.order_hbm, ...), custom_call_target="tpu_custom_call" | custom-call | tf_op jit(solution)/shard_map/pallas_call | solution.py:319
  49.2 1.4 %copy.9 = f32[2,12,192]{2,0,1:T(2,128)} copy(f32[2,12,192]{2,1,0:T(8,128)} %shard_map.82) | data formatting | bytes 36864 | tf_op jit(solution)/shard_map/pallas_call | solution.py:319

commit v4 on v3

--- a/solution.py
+++ b/solution.py
@@ -13,6 +13,7 @@
 BF16 = jnp.bfloat16
 NO = 8
 NE = 64
+NB = 32
 NG = 384
 PTS = 4096
 HALF = PTS // 2
@@ -21,7 +22,7 @@
 GZ = 32
 COLS = 2 * NG
 OWN = COLS // 2
-PAIRS = NO * NE
+PAIRS = NO * NB
 BLOCKS = (0, 1, 6, 7, 2, 8, 3, 4, 9, 10, 5, 11)
 PIECES = tuple((slot, part) for slot in range(2) for part in range(4)) + tuple(
     (slot, part) for part in range(4) for slot in (2, 3)
@@ -52,9 +53,9 @@
 def kernel(
     occ_hbm, emp_hbm, oe_hbm, ee_hbm, partner_hbm, wave_hbm, order_hbm, yz_hbm, out_ref,
     oe_ref, ee_ref, partner_ref, wave_ref, order_ref,
-    shift0, shift1, oe_src, oe_shift, efull, osel, ofull, yz, wtab, utab, vtab, ybuf, proj, ordering, left_t, right,
+    shift0, shift1, oe_src, oe_shift, efull, osel, ofull, yz, wtab, utab, vtab, ybuf, proj, ordering, left_t, right, lefts,
     ga, gb, ra, rb, ta, tb, sa, sb, qa, qb, fa, fb, st, r3,
-    zsend, zrecv, gsend, grecv, rsend, rrecv, fsend, frecv, lsem,
+    zsend, zrecv, gsend, grecv, rsend, rrecv, fsend, frecv, esend, erecv, lsem,
 ):
     shift = (shift0, shift1)
     ka, row = lax.axis_index("ka"), lax.axis_index("row")
@@ -65,13 +66,14 @@
         return (z_ * 8 + xh_ * 4 + y_, xl_ * 2 + core_)
 
     sibling = device(z, xh, y, xl, 1 - core)
+    diagonal = device(z, xh, y, 1 - xl, 1 - core)
     beyond = device(z, 1 - xh, y, xl, core)
     y_peer = [device(z, xh, (y + d) % 4, xl, core) for d in range(1, 4)]
     z_peer = [[device((z + d) % 8, xh, y, xl if r == 0 else 1 - xl, core) for r in range(2)] for d in range(8)]
     across = z_peer[0][1]
 
     barrier = pltpu.get_barrier_semaphore()
-    peers = [z_peer[d][r] for d in (4, 3, 5, 2, 6, 1, 7) for r in range(2)] + [beyond] + y_peer + [across, sibling]
+    peers = [z_peer[d][r] for d in (4, 3, 5, 2, 6, 1, 7) for r in range(2)] + [beyond] + y_peer + [diagonal, across, sibling]
     for peer in peers:
         pl.semaphore_signal(barrier, inc=1, device_id=peer, device_id_type=MESH)
 
@@ -81,9 +83,10 @@
     ):
         small.append(pltpu.make_async_copy(src, dst, lsem.at[number]))
     local = []
+    bands = [pl.ds(pl.multiple_of(c * NB, NB), NB) for c in (core, 1 - core)]
     points = [pl.ds(part * QUART, QUART) for part in range(4)]
     for part in range(4):
-        local.append(pltpu.make_async_copy(emp_hbm.at[0, :, points[part]], efull.at[0, part], lsem.at[6 + part]))
+        local.append(pltpu.make_async_copy(emp_hbm.at[0, bands[0], points[part]], efull.at[0, part], lsem.at[6 + part]))
     for copy in small + local:
         copy.start()
     small[0].wait()
@@ -105,20 +108,22 @@
         sent.append(copy)
         return copy
 
-    shifts, theirs, beside = [[], []], [], []
+    shifts, theirs, oblique, beside = [[], []], [], [], []
 
     def cross(part):
-        theirs.append(send(emp_hbm.at[0, :, points[part]], efull.at[2, part], gsend, grecv, part, across))
+        theirs.append(send(emp_hbm.at[0, bands[0], points[part]], efull.at[2, part], gsend, grecv, part, across))
+        oblique.append(send(emp_hbm.at[0, bands[1], points[part]], efull.at[3, part], gsend, grecv, 8 + part, diagonal))
 
     for half in range(2):
         for s in (2, 1, 3):
             src = occ_hbm.at[0, :, pl.ds(half * HALF, HALF)]
             shifts[half].append(send(src, shift[half].at[s - 1], zsend, zrecv, half * 3 + s - 1, z_peer[2 * s][0]))
-        cross(half)
+    cross(0)
+    cross(1)
     for s in range(1, 4):
         shifts[1].append(send(oe_src, oe_shift.at[s - 1], zsend, zrecv, 5 + s, z_peer[2 * s][0]))
     for part in range(4):
-        beside.append(send(emp_hbm.at[0, :, points[part]], efull.at[1, part], gsend, grecv, 4 + part, sibling))
+        beside.append(send(emp_hbm.at[0, bands[1], points[part]], efull.at[1, part], gsend, grecv, 4 + part, sibling))
 
     for copy in small[1:]:
         copy.wait()
@@ -156,11 +161,7 @@
         return carry
 
     steps = [jnp.clip(partner_ref[q, 0] // 16, 1, 3) - 1 for q in range(2)]
-    passed, passed_occ, occ_beside, occ_across = [], [], [], []
-
-    def pass_on(part):
-        theirs[part].wait_recv()
-        passed.append(send(efull.at[2, part], efull.at[3, part], gsend, grecv, 8 + part, sibling))
+    passed_occ, occ_beside, occ_across = [], [], []
 
     def pass_occ(half):
         occ_across[half].wait_recv()
@@ -193,12 +194,10 @@
     lax.fori_loop(0, 16, fill, 0)
     select(0)
     cross(2)
-    pass_on(0)
     lax.fori_loop(16, 32, fill, 0)
     select(1)
     cross(3)
     pass_occ(0)
-    pass_on(1)
     for part in range(4):
         local[part].wait()
         project(part)
@@ -209,33 +208,44 @@
         project(4 + part)
     proj[...] = gathered(0, 8)
     pass_occ(1)
-    pass_on(2)
     ordering[...] = jnp.where(
         lax.broadcasted_iota(jnp.int32, (COLS, COLS), 0) == order_ref[...], 1.0, 0.0
     ).astype(BF16)
 
     oe = jnp.where(xl == 0, oe_shift[steps[0]], oe_shift[steps[1]])
-    pick = lax.broadcasted_iota(jnp.int32, (NE, NE), 1) == lax.broadcasted_iota(jnp.int32, (NE, NE), 0)
-    ee = jnp.broadcast_to(ee_ref[...].astype(F32), (NE, NE))
-    ee = jnp.sum(jnp.where(pick, ee, 0.0), axis=1, keepdims=True)
-    weight = jnp.concatenate([1.0 / (ee - oe[v : v + 1, 0:1]) for v in range(NO)], axis=0)
-
-    for part in range(4):
+    ee = jnp.broadcast_to(ee_ref[...].astype(F32), (NB, NE))
+    spot = lax.broadcasted_iota(jnp.int32, (NB, NE), 1) - lax.broadcasted_iota(jnp.int32, (NB, NE), 0)
+    weights = []
+    for c in (core, 1 - core):
+        level = jnp.sum(jnp.where(spot == c * NB, ee, 0.0), axis=1, keepdims=True)
+        weights.append(jnp.concatenate([1.0 / (level - oe[v : v + 1, 0:1]) for v in range(NO)], axis=0))
+
+    for part in range(4):
+        theirs[part].wait_recv()
         project(8 + 2 * part)
-        passed[part].wait_recv()
+        oblique[part].wait_recv()
         if part % 2 == 0:
             passed_occ[part // 2].wait_recv()
         project(9 + 2 * part)
         if part == 1:
-            pass_on(3)
-        if part < 3:
-            proj[...] = proj[...] + gathered(8 + 2 * part, 10 + 2 * part)
-    proj[...] = (proj[...] + gathered(14, 16)) * (1.0 / (4 * PTS))
-    left = proj[...].astype(BF16)
-    right[...] = (weight * proj[:, pl.ds(pl.multiple_of(core * OWN, OWN), OWN)]).astype(BF16)
-    left_t[...] = lax.dot_general(
-        ordering[...], left, (((1,), (1,)), ((), ())), preferred_element_type=F32
-    ).astype(BF16)
+            proj[...] = proj[...] + gathered(8, 12)
+    exchange = []
+    cols = pl.ds(pl.multiple_of(core * OWN, OWN), OWN)
+    for part in range(2):
+        rows = slice(part * 128, part * 128 + 128)
+        last = jnp.dot(ybuf[rows, 3072:4096], wtab[3072:4096, :], preferred_element_type=F32)
+        lefts[0, part] = ((proj[rows, :] + last) * (1.0 / (4 * PTS))).astype(BF16)
+        exchange.append(send(lefts.at[0, part], lefts.at[1, part], esend, erecv, part, sibling))
+    for who in range(2):
+        for part in range(2):
+            if who:
+                exchange[part].wait_recv()
+            first = who * PAIRS + part * 128
+            weight = weights[who][part * 128 : part * 128 + 128]
+            right[first : first + 128, :] = (weight * lefts[who, part, :, cols].astype(F32)).astype(BF16)
+            left_t[:, first : first + 128] = lax.dot_general(
+                ordering[...], lefts[who, part], (((1,), (1,)), ((), ())), preferred_element_type=F32
+            ).astype(BF16)
 
     def a_block(y_):
         rows = pl.ds(pl.multiple_of(y_ * 96, 96), 96)
@@ -331,7 +341,7 @@
             pltpu.VMEM((3, NO, HALF), BF16),
             pltpu.VMEM((NO, 128), F32),
             pltpu.VMEM((3, NO, 128), F32),
-            pltpu.VMEM((4, 4, NE, QUART), BF16),
+            pltpu.VMEM((4, 4, NB, QUART), BF16),
             pltpu.VMEM((2, 2, NO, HALF), BF16),
             pltpu.VMEM((4, 2, NO, HALF), BF16),
             pltpu.VMEM((YZ, 128), BF16),
@@ -341,8 +351,9 @@
             pltpu.VMEM((PAIRS, 4096), BF16),
             pltpu.VMEM((PAIRS, COLS), F32),
             pltpu.VMEM((COLS, COLS), BF16),
-            pltpu.VMEM((COLS, PAIRS), BF16),
-            pltpu.VMEM((PAIRS, OWN), BF16),
+            pltpu.VMEM((COLS, 2 * PAIRS), BF16),
+            pltpu.VMEM((2 * PAIRS, OWN), BF16),
+            pltpu.VMEM((2, 2, 128, COLS), BF16),
             pltpu.VMEM((3, 96, OWN), BF16),
             pltpu.VMEM((192, OWN), BF16),
             pltpu.VMEM((3, 96, OWN), BF16),
@@ -357,7 +368,7 @@
             pltpu.VMEM((64, OWN), F32),
             pltpu.VMEM((8, 2, 16, 256), BF16),
             pltpu.VMEM((8, 2, 16, 256), BF16),
-            dma((9,)), dma((9,)), dma((18,)), dma((18,)), dma((8,)), dma((8,)), dma((16,)), dma((16,)), dma((10,)),
+            dma((9,)), dma((9,)), dma((18,)), dma((18,)), dma((8,)), dma((8,)), dma((16,)), dma((16,)), dma((2,)), dma((2,)), dma((10,)),
         ],
         compiler_params=pltpu.CompilerParams(
             collective_id=0, has_side_effects=True, vmem_limit_bytes=60 * 1024 * 1024

time: 50.7 us -> 48.4 us (0.955)
  the two profiles are of different devices: /device:TPU:2 before, /device:TPU:1 now
where the time goes in v4:
time: 48.4 us; the launch traced here: 47.7 us
  Pallas kernels  46.3 us (96%)
  local copies, waits for them, and re-layouts  1.39 us (3%)
    pallas_call x1, Pallas kernels, per_device(): pl.pallas_call(kernel, out_shape=jax.ShapeDtypeStruct((2, 12, 192), F32),...  46.3 us
    pallas_call x1, local copies, waits for them, and re-layouts, per_device(): pl.pallas_call(kernel, out_shape=jax.ShapeDtypeStruct((2, 12, 192), F32),...  1.39 us

profile of v4, /device:TPU:1, one launch (start us, length us, event | category | flops | bytes accessed | tf_op | source)
XLA Modules:
  0.0 47.7 jit_solution(11419504340455377445)
XLA Ops:
  0.0 46.3 %shard_map.82 = f32[2,12,192]{2,1,0:T(8,128)} custom-call(bf16[1,8,4096]{2,1,0:T(8,128)(2,1)} %occ_hbm.1, bf16[1,64,4096]{2,1,0:T(8,128)(2,1)} %emp_hbm.1, bf16[1,8]{1,0:T(2,128)(2,1)} %oe_hbm.1, bf16[1,64]{1,0:T(2,128)(2,1)} %ee_hbm.1, s32[2,64]{1,0:T(2,128)} %partner_hbm.1, s32[3,2,384]{2,1,0:T(2,128)} %bitcast.1, s32[1,768]{1,0:T(1,128)} %constant.4.clone.order_hbm, ...), custom_call_target="tpu_custom_call" | custom-call | tf_op jit(solution)/shard_map/pallas_call | solution.py:329
  46.3 1.4 %copy.9 = f32[2,12,192]{2,0,1:T(2,128)} copy(f32[2,12,192]{2,1,0:T(8,128)} %shard_map.82) | data formatting | bytes 36864 | tf_op jit(solution)/shard_map/pallas_call | solution.py:329

commit v5 on v4

--- a/solution.py
+++ b/solution.py
@@ -229,23 +229,19 @@
         project(9 + 2 * part)
         if part == 1:
             proj[...] = proj[...] + gathered(8, 12)
-    exchange = []
+        if part == 2:
+            proj[...] = proj[...] + gathered(12, 14)
     cols = pl.ds(pl.multiple_of(core * OWN, OWN), OWN)
-    for part in range(2):
-        rows = slice(part * 128, part * 128 + 128)
-        last = jnp.dot(ybuf[rows, 3072:4096], wtab[3072:4096, :], preferred_element_type=F32)
-        lefts[0, part] = ((proj[rows, :] + last) * (1.0 / (4 * PTS))).astype(BF16)
-        exchange.append(send(lefts.at[0, part], lefts.at[1, part], esend, erecv, part, sibling))
+    lefts[0] = ((proj[...] + gathered(14, 16)) * (1.0 / (4 * PTS))).astype(BF16)
+    exchange = send(lefts.at[0], lefts.at[1], esend, erecv, 0, sibling)
     for who in range(2):
-        for part in range(2):
-            if who:
-                exchange[part].wait_recv()
-            first = who * PAIRS + part * 128
-            weight = weights[who][part * 128 : part * 128 + 128]
-            right[first : first + 128, :] = (weight * lefts[who, part, :, cols].astype(F32)).astype(BF16)
-            left_t[:, first : first + 128] = lax.dot_general(
-                ordering[...], lefts[who, part], (((1,), (1,)), ((), ())), preferred_element_type=F32
-            ).astype(BF16)
+        if who:
+            exchange.wait_recv()
+        span = slice(who * PAIRS, who * PAIRS + PAIRS)
+        right[span, :] = (weights[who] * lefts[who, :, cols].astype(F32)).astype(BF16)
+        left_t[:, span] = lax.dot_general(
+            ordering[...], lefts[who], (((1,), (1,)), ((), ())), preferred_element_type=F32
+        ).astype(BF16)
 
     def a_block(y_):
         rows = pl.ds(pl.multiple_of(y_ * 96, 96), 96)
@@ -353,7 +349,7 @@
             pltpu.VMEM((COLS, COLS), BF16),
             pltpu.VMEM((COLS, 2 * PAIRS), BF16),
             pltpu.VMEM((2 * PAIRS, OWN), BF16),
-            pltpu.VMEM((2, 2, 128, COLS), BF16),
+            pltpu.VMEM((2, PAIRS, COLS), BF16),
             pltpu.VMEM((3, 96, OWN), BF16),
             pltpu.VMEM((192, OWN), BF16),
             pltpu.VMEM((3, 96, OWN), BF16),
@@ -368,7 +364,7 @@
             pltpu.VMEM((64, OWN), F32),
             pltpu.VMEM((8, 2, 16, 256), BF16),
             pltpu.VMEM((8, 2, 16, 256), BF16),
-            dma((9,)), dma((9,)), dma((18,)), dma((18,)), dma((8,)), dma((8,)), dma((16,)), dma((16,)), dma((2,)), dma((2,)), dma((10,)),
+            dma((9,)), dma((9,)), dma((18,)), dma((18,)), dma((8,)), dma((8,)), dma((16,)), dma((16,)), dma((1,)), dma((1,)), dma((10,)),
         ],
         compiler_params=pltpu.CompilerParams(
             collective_id=0, has_side_effects=True, vmem_limit_bytes=60 * 1024 * 1024

time: 48.4 us -> 48.1 us (level)
  no operation moved by 1% of the time
where the time goes in v5:
time: 48.1 us; the launch traced here: 47.5 us
  Pallas kernels  46.1 us (96%)
  local copies, waits for them, and re-layouts  1.39 us (3%)
    pallas_call x1, Pallas kernels, per_device(): pl.pallas_call(kernel, out_shape=jax.ShapeDtypeStruct((2, 12, 192), F32),...  46.1 us
    pallas_call x1, local copies, waits for them, and re-layouts, per_device(): pl.pallas_call(kernel, out_shape=jax.ShapeDtypeStruct((2, 12, 192), F32),...  1.39 us

profile of v5, /device:TPU:1, one launch (start us, length us, event | category | flops | bytes accessed | tf_op | source)
XLA Modules:
  0.0 47.5 jit_solution(9703513200440877476)
XLA Ops:
  0.0 46.1 %shard_map.82 = f32[2,12,192]{2,1,0:T(8,128)} custom-call(bf16[1,8,4096]{2,1,0:T(8,128)(2,1)} %occ_hbm.1, bf16[1,64,4096]{2,1,0:T(8,128)(2,1)} %emp_hbm.1, bf16[1,8]{1,0:T(2,128)(2,1)} %oe_hbm.1, bf16[1,64]{1,0:T(2,128)(2,1)} %ee_hbm.1, s32[2,64]{1,0:T(2,128)} %partner_hbm.1, s32[3,2,384]{2,1,0:T(2,128)} %bitcast.1, s32[1,768]{1,0:T(1,128)} %constant.4.clone.order_hbm, ...), custom_call_target="tpu_custom_call" | custom-call | tf_op jit(solution)/shard_map/pallas_call | solution.py:325
  46.1 1.4 %copy.9 = f32[2,12,192]{2,0,1:T(2,128)} copy(f32[2,12,192]{2,1,0:T(8,128)} %shard_map.82) | data formatting | bytes 36864 | tf_op jit(solution)/shard_map/pallas_call | solution.py:325

commit v6 on v2

v6 whole, which is shorter than its diff:
```python
import math

import jax
import jax.numpy as jnp
import numpy as np
from jax import lax
from jax.experimental import pallas as pl
from jax.experimental.pallas import tpu as pltpu
from jax.sharding import PartitionSpec as P

MESH = pl.DeviceIdType.MESH
F32 = jnp.float32
BF16 = jnp.bfloat16
NO = 8
NB = 32
NG = 384
PTS = 4096
HALF = PTS // 2
YZ = 512
GZ = 32
COLS = 2 * NG
PAIRS = NO * NB
OWN = COLS // 2
BLOCKS = (0, 1, 3, 4, 2, 5, 6, 7, 9, 10, 8, 11)
PIECES = ((0, 0), (0, 1), (1, 0), (1, 1), (2, 0), (3, 0), (2, 1), (3, 1))
DIST = (2, 1, 3)


def yz_table():
    point = np.arange(YZ)
    y, z = point // GZ, point % GZ
    table = np.zeros((YZ, 128), np.float64)
    for g1 in range(-4, 5):
        for g2 in range(5):
            turn = 2 * math.pi * ((g1 * y * 2 + g2 * z) % 32) / 32
            column = (g1 + 4) * 5 + g2
            table[:, column] = np.cos(turn)
            table[:, 64 + column] = np.sin(turn)
    return table.astype(np.float32)


def row_order():
    a = np.concatenate([np.arange(64) + 64 * block for block in BLOCKS])
    z, xh, y, i = a // 96, a // 48 % 2, a // 12 % 4, a % 12
    first = xh * 192 + y * 48 + (z % 4) * 12 + i
    second = 384 + y * 96 + xh * 48 + (z % 4) * 12 + i
    return np.where(z < 4, first, second).astype(np.int32).reshape(1, COLS)


def kernel(
    occ_hbm, emp_hbm, oe_hbm, ee_hbm, partner_hbm, wave_hbm, order_hbm, yz_hbm, out_ref,
    oe_ref, ee_ref, partner_ref, wave_ref, order_ref,
    shift0, shift1, oe_src, oe_shift, efull, osel, ofull, yz, wtab, utab, vtab, ybuf, proj, ordering, left_t, right,
    ga, gb, ra, rb, ta, tb, sa, sb, qa, qb, fa, fb, st, r3,
    zsend, zrecv, gsend, grecv, rsend, rrecv, fsend, frecv, lsem,
):
    shift = (shift0, shift1)
    ka, row = lax.axis_index("ka"), lax.axis_index("row")
    z, xh, y = ka // 8, ka // 4 % 2, ka % 4
    xl, core = row // 2, row % 2
    x = xh * 2 + xl

    def device(z_, x_, y_, core_):
        return (z_ * 8 + (x_ // 2) * 4 + y_, (x_ % 2) * 2 + core_)

    sibling = (ka, xl * 2 + 1 - core)
    across = (ka, (1 - xl) * 2 + core)
    diagonal = (ka, (1 - xl) * 2 + 1 - core)
    x_peer = [device(z, (x + d) % 4, y, core) for d in range(1, 4)]
    y_peer = [device(z, x, (y + d) % 4, core) for d in range(1, 4)]
    z_peer = [[device((z + d) % 8, x, y, core if r == 0 else 1 - core) for r in range(2)] for d in range(8)]

    barrier = pltpu.get_barrier_semaphore()
    peers = [sibling, diagonal] + x_peer + y_peer + [z_peer[d][r] for d in range(1, 8) for r in range(2)]
    for peer in peers:
        pl.semaphore_signal(barrier, inc=1, device_id=peer, device_id_type=MESH)

    small = []
    for number, (src, dst) in enumerate(
        [(oe_hbm, oe_ref), (wave_hbm, wave_ref), (ee_hbm, ee_ref), (partner_hbm, partner_ref), (order_hbm, order_ref), (yz_hbm, yz)]
    ):
        small.append(pltpu.make_async_copy(src, dst, lsem.at[number]))
    local = []
    own_bands = pl.ds(pl.multiple_of(xl * NB, NB), NB)
    their_bands = pl.ds(pl.multiple_of((1 - xl) * NB, NB), NB)
    points = [pl.ds(half * HALF, HALF) for half in range(2)]
    for half in range(2):
        local.append(pltpu.make_async_copy(emp_hbm.at[0, own_bands, points[half]], efull.at[0, half], lsem.at[6 + half]))
    for copy in small + local:
        copy.start()
    small[0].wait()

    eye = lax.broadcasted_iota(jnp.int32, (NO, NO), 0) == lax.broadcasted_iota(jnp.int32, (NO, NO), 1)
    levels = jnp.broadcast_to(oe_ref[...].astype(F32), (NO, NO))
    column = jnp.sum(jnp.where(eye, levels, 0.0), axis=1, keepdims=True)
    oe_src[...] = jnp.broadcast_to(column, (NO, 128))
    pl.semaphore_wait(barrier, len(peers))

    sent = []

    def send(src, dst, sends, recvs, index, peer):
        copy = pltpu.make_async_remote_copy(
            src_ref=src, dst_ref=dst, send_sem=sends.at[index], recv_sem=recvs.at[index],
            device_id=peer, device_id_type=MESH,
        )
        copy.start()
        sent.append(copy)
        return copy

    shifts, theirs, beside = [[], []], [], []
    for half in range(2):
        for s in (2, 1, 3):
            shifts[half].append(
                send(occ_hbm.at[0, :, points[half]], shift[half].at[s - 1], zsend, zrecv, half * 3 + s - 1, z_peer[2 * s][0])
            )
        theirs.append(send(emp_hbm.at[0, their_bands, points[half]], efull.at[2, half], gsend, grecv, half, across))
    for s in range(1, 4):
        shifts[1].append(send(oe_src, oe_shift.at[s - 1], zsend, zrecv, 5 + s, z_peer[2 * s][0]))
    for half in range(2):
        beside.append(send(emp_hbm.at[0, own_bands, points[half]], efull.at[1, half], gsend, grecv, 2 + half, sibling))

    for copy in small[1:]:
        copy.wait()

    def kept(line):
        both = jnp.concatenate([line, line], axis=1)
        return jnp.concatenate([both[:, 64 * block : 64 * block + 64] for block in BLOCKS], axis=1)

    g0, g1, g2 = [
        kept(jnp.where(core == 0, wave_ref[axis, 0:1, :], wave_ref[axis, 1:2, :])) for axis in range(3)
    ]
    flip = jnp.where(g2 < 0, -1, 1)
    group = (flip * g1 + 4) * 5 + flip * g2
    index = lax.broadcasted_iota(jnp.int32, (32, COLS), 0)
    piece = index >> 2
    slot = jnp.where(piece < 4, piece >> 1, 2 + (piece & 1))
    half_of = jnp.where(piece < 4, piece & 1, (piece - 4) >> 1)
    src_core = (core + slot) & 1
    src_xl = (xl + (slot >> 1)) & 1
    plane = (src_xl * 2 + src_core) * 8 + half_of * 4 + (index & 3)
    lane = lax.broadcasted_iota(jnp.int32, (32, COLS), 1)
    quarter = jnp.where(lane < OWN, 0, 8)
    turn = ((g0 * plane - quarter) & 31).astype(F32) * (2.0 * math.pi / 32)
    utab[...] = jnp.cos(turn)
    vtab[...] = jnp.sin(turn) * (-flip).astype(F32)
    chosen = lax.broadcasted_iota(jnp.int32, (64, COLS), 0) == group

    def fill(i, carry):
        u = utab[pl.ds(i, 1), :]
        v = vtab[pl.ds(i, 1), :]
        base = pl.multiple_of(i * 128, 128)
        wtab[pl.ds(base, 64), :] = jnp.where(chosen, u, 0.0).astype(BF16)
        wtab[pl.ds(base + 64, 64), :] = jnp.where(chosen, v, 0.0).astype(BF16)
        return carry

    lax.fori_loop(0, 32, fill, 0)

    steps = [jnp.clip(partner_ref[q, 0] // 16, 1, 3) - 1 for q in range(2)]
    passed, gathers = [], [[], []]

    def pass_on(half):
        theirs[half].wait_recv()
        passed.append(send(efull.at[2, half], efull.at[3, half], gsend, grecv, 4 + half, sibling))

    def select(half):
        for copy in shifts[half]:
            copy.wait_recv()
        for q in range(2):
            osel[half, q] = shift[half][steps[q]]
        gathers[half].append(send(osel.at[half, 1 - core], ofull.at[1, half], gsend, grecv, 6 + half, sibling))
        gathers[half].append(send(osel.at[half, core], ofull.at[2, half], gsend, grecv, 8 + half, across))
        gathers[half].append(send(osel.at[half, 1 - core], ofull.at[3, half], gsend, grecv, 10 + half, diagonal))
        ofull[0, half] = osel[half, core]

    def project(number):
        slot, half = PIECES[number]
        for i in range(4):
            lanes = slice(i * YZ, (i + 1) * YZ)
            e = efull[slot, half, :, lanes].astype(F32)
            o = ofull[slot, half, :, lanes].astype(F32)
            density = jnp.concatenate([(o[v : v + 1] * e).astype(BF16) for v in range(NO)], axis=0)
            part = jnp.dot(density, yz[...], preferred_element_type=F32)
            first = (number * 4 + i) * 128
            ybuf[:, first : first + 128] = part.astype(BF16)

    def gathered(begin, end):
        return jnp.dot(ybuf[:, begin * 512 : end * 512], wtab[begin * 512 : end * 512, :], preferred_element_type=F32)

    pass_on(0)
    select(0)
    ordering[...] = jnp.where(
        lax.broadcasted_iota(jnp.int32, (COLS, COLS), 0) == order_ref[...], 1.0, 0.0
    ).astype(BF16)
    pass_on(1)
    select(1)

    oe = jnp.where(core == 0, oe_shift[steps[0]], oe_shift[steps[1]])
    pick = lax.broadcasted_iota(jnp.int32, (NB, 2 * NB), 1) == lax.broadcasted_iota(jnp.int32, (NB, 2 * NB), 0) + xl * NB
    ee = jnp.broadcast_to(ee_ref[...].astype(F32), (NB, 2 * NB))
    ee = jnp.sum(jnp.where(pick, ee, 0.0), axis=1, keepdims=True)
    weight = jnp.concatenate([1.0 / (ee - oe[v : v + 1, 0:1]) for v in range(NO)], axis=0)

    for half in range(2):
        local[half].wait()
        project(half)
    for half in range(2):
        beside[half].wait_recv()
        gathers[half][0].wait_recv()
        project(2 + half)
    proj[...] = gathered(0, 4)
    for half in range(2):
        gathers[half][1].wait_recv()
        project(4 + 2 * half)
        gathers[half][2].wait_recv()
        passed[half].wait_recv()
        project(5 + 2 * half)
        if half == 0:
            proj[...] = proj[...] + gathered(4, 6)

    value = (proj[...] + gathered(6, 8)) * (1.0 / (4 * PTS))
    left = value.astype(BF16)
    right[...] = (weight * value).astype(BF16)
    left_t[...] = lax.dot_general(
        ordering[...], left, (((1,), (1,)), ((), ())), preferred_element_type=F32
    ).astype(BF16)

    def a_block(x_):
        rows = pl.ds(pl.multiple_of(x_ // 2 * 192, 192), 192)
        cols = pl.ds(pl.multiple_of(x_ % 2 * OWN, OWN), OWN)
        return jnp.dot(left_t[rows, :], right[:, cols], preferred_element_type=F32)

    def b_block(y_):
        rows = pl.ds(pl.multiple_of(384 + y_ * 96, 96), 96)
        return jnp.dot(left_t[rows, :], right[...], preferred_element_type=F32)

    first_a, first_b, second_a, second_b = [], [], [], []
    for d in DIST:
        ga[d - 1] = a_block((x + d) % 4).astype(BF16)
        first_a.append(send(ga.at[d - 1], ra.at[d - 1], rsend, rrecv, d - 1, x_peer[d - 1]))
        gb[d - 1] = b_block((y + d) % 4).astype(BF16)
        first_b.append(send(gb.at[d - 1], rb.at[d - 1], rsend, rrecv, d + 2, y_peer[d - 1]))
    ta[...] = a_block(x)
    tb[...] = b_block(y)

    for copy in first_a:
        copy.wait_recv()
    total = ta[...]
    for d in range(3):
        total = total + ra[d].astype(F32)
    ta[...] = total
    sa[...] = total.astype(BF16)
    for d in DIST:
        rows = pl.ds(pl.multiple_of((y + d) % 4 * 48, 48), 48)
        second_a.append(send(sa.at[rows], qa.at[d - 1], rsend, rrecv, d + 5, y_peer[d - 1]))
    for copy in first_b:
        copy.wait_recv()
    total = tb[...]
    for d in range(3):
        total = total + rb[d].astype(F32)
    tb[...] = total
    sb[...] = total.astype(BF16)
    for d in DIST:
        to = (x + d) % 4
        rows = pl.ds(pl.multiple_of(to // 2 * 48, 48), 48)
        cols = pl.ds(pl.multiple_of(to % 2 * OWN, OWN), OWN)
        second_b.append(send(sb.at[rows, cols], qb.at[d - 1], rsend, rrecv, d + 8, x_peer[d - 1]))

    third = {}

    def ready(source, first):
        for to in range(4):
            rows = slice(to * 12, to * 12 + 16)
            tail = source[rows, 256:384].astype(BF16)
            for side in range(2):
                st[first + to, side, :, 0:128] = source[rows, side * 128 : side * 128 + 128].astype(BF16)
                st[first + to, side, :, 128:256] = tail

    for copy in second_a:
        copy.wait_recv()
    total = ta[pl.ds(pl.multiple_of(y * 48, 48), 48), :]
    for d in range(3):
        total = total + qa[d].astype(F32)
    fa[0:48, :] = total
    ready(fa, 0)
    for copy in second_b:
        copy.wait_recv()
    total = tb[pl.ds(pl.multiple_of(xh * 48, 48), 48), pl.ds(pl.multiple_of(xl * OWN, OWN), OWN)]
    for d in range(3):
        total = total + qb[d].astype(F32)
    fb[0:48, :] = total
    ready(fb, 4)
    for d in (4, 3, 5, 2, 6, 1, 7, 0):
        for r in range(2):
            if d or r:
                side = core if r == 0 else 1 - core
                third[d, r] = send(st.at[(z + d) % 8, side], r3.at[d, r], fsend, frecv, d * 2 + r, z_peer[d][r])
    mine = st[z, core].astype(F32)
    other = jnp.zeros((16, 256), F32)
    for d in (0, 1, 7, 2, 6, 3, 5, 4):
        if d:
            third[d, 0].wait_recv()
            mine = mine + r3[d, 0].astype(F32)
        third[d, 1].wait_recv()
        other = other + r3[d, 1].astype(F32)
    for q in range(2):
        total = jnp.where(core == q, mine, other)[0:12]
        out_ref[q, :, 0:128] = total[:, 0:128]
        out_ref[q, :, 128:192] = jnp.where(core == 0, total[:, 128:192], total[:, 192:256])
    for copy in sent:
        copy.wait_send()


def per_device(occupied, empty, occ_energy, emp_energy, partner, gvecs):
    waves = jnp.transpose(gvecs, (2, 0, 1))
    hbm = pl.BlockSpec(memory_space=pl.ANY)
    dma = pltpu.SemaphoreType.DMA
    return pl.pallas_call(
        kernel,
        out_shape=jax.ShapeDtypeStruct((2, 12, 192), F32),
        in_specs=[hbm] * 8,
        out_specs=pl.BlockSpec(memory_space=pltpu.VMEM),
        scratch_shapes=[
            pltpu.VMEM((1, NO), BF16),
            pltpu.VMEM((1, 2 * NB), BF16),
            pltpu.SMEM((2, 64), jnp.int32),
            pltpu.VMEM((3, 2, NG), jnp.int32),
            pltpu.VMEM((1, COLS), jnp.int32),
            pltpu.VMEM((3, NO, HALF), BF16),
            pltpu.VMEM((3, NO, HALF), BF16),
            pltpu.VMEM((NO, 128), F32),
            pltpu.VMEM((3, NO, 128), F32),
            pltpu.VMEM((4, 2, NB, HALF), BF16),
            pltpu.VMEM((2, 2, NO, HALF), BF16),
            pltpu.VMEM((4, 2, NO, HALF), BF16),
            pltpu.VMEM((YZ, 128), BF16),
            pltpu.VMEM((4096, COLS), BF16),
            pltpu.VMEM((32, COLS), F32),
            pltpu.VMEM((32, COLS), F32),
            pltpu.VMEM((PAIRS, 4096), BF16),
            pltpu.VMEM((PAIRS, COLS), F32),
            pltpu.VMEM((COLS, COLS), BF16),
            pltpu.VMEM((COLS, PAIRS), BF16),
            pltpu.VMEM((PAIRS, COLS), BF16),
            pltpu.VMEM((3, 192, OWN), BF16),
            pltpu.VMEM((3, 96, COLS), BF16),
            pltpu.VMEM((3, 192, OWN), BF16),
            pltpu.VMEM((3, 96, COLS), BF16),
            pltpu.VMEM((192, OWN), F32),
            pltpu.VMEM((96, COLS), F32),
            pltpu.VMEM((192, OWN), BF16),
            pltpu.VMEM((96, COLS), BF16),
            pltpu.VMEM((3, 48, OWN), BF16),
            pltpu.VMEM((3, 48, OWN), BF16),
            pltpu.VMEM((64, OWN), F32),
            pltpu.VMEM((64, OWN), F32),
            pltpu.VMEM((8, 2, 16, 256), BF16),
            pltpu.VMEM((8, 2, 16, 256), BF16),
            dma((9,)), dma((9,)), dma((12,)), dma((12,)), dma((12,)), dma((12,)), dma((16,)), dma((16,)), dma((8,)),
        ],
        compiler_params=pltpu.CompilerParams(
            collective_id=0, has_side_effects=True, vmem_limit_bytes=60 * 1024 * 1024
        ),
    )(
        occupied, empty, occ_energy, emp_energy, partner, waves,
        jnp.asarray(row_order()), jnp.asarray(yz_table()).astype(BF16),
    )


def solution(mesh):
    placed = (P("ka", None, "row"), P("ka", None, "row"), P("ka", None), P("ka", None), P(), P())
    return jax.shard_map(
        per_device, mesh=mesh, in_specs=placed, out_specs=P(None, "ka", "row"), check_vma=False
    )
```

time: 49.8 us -> 49 us (0.984)
  Pallas kernels: 48.3 us -> 47.5 us
    pallas_call x0 -> x1, local copies, waits for them, and re-layouts: none -> 1.39 us  [per_device(): pl.pallas_call(kernel, out_shape=jax.ShapeDtypeStruct((2, 12, 192), F32),...]
    unnamed x1 -> x0, local copies, waits for them, and re-layouts: 1.35 us -> none
    pallas_call x1, Pallas kernels: 48.3 us -> 47.5 us  [per_device(): pl.pallas_call(kernel, out_shape=jax.ShapeDtypeStruct((2, 12, 192), F32),...]
where the time goes in v6:
time: 49 us; the launch traced here: 48.9 us
  Pallas kernels  47.5 us (97%)
  local copies, waits for them, and re-layouts  1.39 us (3%)
    pallas_call x1, Pallas kernels, per_device(): pl.pallas_call(kernel, out_shape=jax.ShapeDtypeStruct((2, 12, 192), F32),...  47.5 us
    pallas_call x1, local copies, waits for them, and re-layouts, per_device(): pl.pallas_call(kernel, out_shape=jax.ShapeDtypeStruct((2, 12, 192), F32),...  1.39 us

profile of v6, /device:TPU:1, one launch (start us, length us, event | category | flops | bytes accessed | tf_op | source)
XLA Modules:
  0.0 48.9 jit_solution(6631043941428707698)
XLA Ops:
  0.0 47.5 %shard_map.82 = f32[2,12,192]{2,1,0:T(8,128)} custom-call(bf16[1,8,4096]{2,1,0:T(8,128)(2,1)} %occ_hbm.1, bf16[1,64,4096]{2,1,0:T(8,128)(2,1)} %emp_hbm.1, bf16[1,8]{1,0:T(2,128)(2,1)} %oe_hbm.1, bf16[1,64]{1,0:T(2,128)(2,1)} %ee_hbm.1, s32[2,64]{1,0:T(2,128)} %partner_hbm.1, s32[3,2,384]{2,1,0:T(2,128)} %bitcast.1, s32[1,768]{1,0:T(1,128)} %constant.4.clone.order_hbm, ...), custom_call_target="tpu_custom_call" | custom-call | tf_op jit(solution)/shard_map/pallas_call | solution.py:317
  47.5 1.4 %copy.9 = f32[2,12,192]{2,0,1:T(2,128)} copy(f32[2,12,192]{2,1,0:T(8,128)} %shard_map.82) | data formatting | bytes 36864 | tf_op jit(solution)/shard_map/pallas_call | solution.py:317

commit v7 on v5

--- a/solution.py
+++ b/solution.py
@@ -163,16 +163,13 @@
     steps = [jnp.clip(partner_ref[q, 0] // 16, 1, 3) - 1 for q in range(2)]
     passed_occ, occ_beside, occ_across = [], [], []
 
-    def pass_occ(half):
-        occ_across[half].wait_recv()
-        passed_occ.append(send(ofull.at[2, half], ofull.at[3, half], gsend, grecv, 16 + half, sibling))
-
     def select(half):
         for copy in shifts[half]:
             copy.wait_recv()
         for q in range(2):
             osel[half, q] = shift[half][steps[q]]
         occ_across.append(send(osel.at[half, 1 - xl], ofull.at[2, half], gsend, grecv, 14 + half, across))
+        passed_occ.append(send(osel.at[half, 1 - xl], ofull.at[3, half], gsend, grecv, 16 + half, diagonal))
         occ_beside.append(send(osel.at[half, xl], ofull.at[1, half], gsend, grecv, 12 + half, sibling))
         ofull[0, half] = osel[half, xl]
 
@@ -197,7 +194,6 @@
     lax.fori_loop(16, 32, fill, 0)
     select(1)
     cross(3)
-    pass_occ(0)
     for part in range(4):
         local[part].wait()
         project(part)
@@ -207,7 +203,6 @@
         beside[part].wait_recv()
         project(4 + part)
     proj[...] = gathered(0, 8)
-    pass_occ(1)
     ordering[...] = jnp.where(
         lax.broadcasted_iota(jnp.int32, (COLS, COLS), 0) == order_ref[...], 1.0, 0.0
     ).astype(BF16)
@@ -221,6 +216,8 @@
         weights.append(jnp.concatenate([1.0 / (level - oe[v : v + 1, 0:1]) for v in range(NO)], axis=0))
 
     for part in range(4):
+        if part % 2 == 0:
+            occ_across[part // 2].wait_recv()
         theirs[part].wait_recv()
         project(8 + 2 * part)
         oblique[part].wait_recv()

time: 48.1 us -> 47.8 us (level)
  no operation moved by 1% of the time
where the time goes in v7:
time: 47.8 us; the launch traced here: 47.2 us
  Pallas kernels  45.8 us (96%)
  local copies, waits for them, and re-layouts  1.39 us (3%)
    pallas_call x1, Pallas kernels, per_device(): pl.pallas_call(kernel, out_shape=jax.ShapeDtypeStruct((2, 12, 192), F32),...  45.8 us
    pallas_call x1, local copies, waits for them, and re-layouts, per_device(): pl.pallas_call(kernel, out_shape=jax.ShapeDtypeStruct((2, 12, 192), F32),...  1.39 us

profile of v7, /device:TPU:1, one launch (start us, length us, event | category | flops | bytes accessed | tf_op | source)
XLA Modules:
  0.0 47.2 jit_solution(17750818065625321551)
XLA Ops:
  0.0 45.8 %shard_map.82 = f32[2,12,192]{2,1,0:T(8,128)} custom-call(bf16[1,8,4096]{2,1,0:T(8,128)(2,1)} %occ_hbm.1, bf16[1,64,4096]{2,1,0:T(8,128)(2,1)} %emp_hbm.1, bf16[1,8]{1,0:T(2,128)(2,1)} %oe_hbm.1, bf16[1,64]{1,0:T(2,128)(2,1)} %ee_hbm.1, s32[2,64]{1,0:T(2,128)} %partner_hbm.1, s32[3,2,384]{2,1,0:T(2,128)} %bitcast.1, s32[1,768]{1,0:T(1,128)} %constant.4.clone.order_hbm, ...), custom_call_target="tpu_custom_call" | custom-call | tf_op jit(solution)/shard_map/pallas_call | solution.py:322
  45.8 1.4 %copy.9 = f32[2,12,192]{2,0,1:T(2,128)} copy(f32[2,12,192]{2,1,0:T(8,128)} %shard_map.82) | data formatting | bytes 36864 | tf_op jit(solution)/shard_map/pallas_call | solution.py:322

commit v8 on v7

--- a/solution.py
+++ b/solution.py
@@ -45,16 +45,14 @@
 def row_order():
     a = np.concatenate([np.arange(64) + 64 * block for block in BLOCKS])
     z, xh, y, i = a // 96, a // 48 % 2, a // 12 % 4, a % 12
-    first = y * 96 + xh * 48 + (z % 4) * 12 + i
-    second = 384 + xh * 192 + y * 48 + (z % 4) * 12 + i
-    return np.where(z < 4, first, second).astype(np.int32).reshape(1, COLS)
+    return (y * 192 + xh * 96 + z * 12 + i).astype(np.int32).reshape(1, COLS)
 
 
 def kernel(
     occ_hbm, emp_hbm, oe_hbm, ee_hbm, partner_hbm, wave_hbm, order_hbm, yz_hbm, out_ref,
     oe_ref, ee_ref, partner_ref, wave_ref, order_ref,
     shift0, shift1, oe_src, oe_shift, efull, osel, ofull, yz, wtab, utab, vtab, ybuf, proj, ordering, left_t, right, lefts,
-    ga, gb, ra, rb, ta, tb, sa, sb, qa, qb, fa, fb, st, r3,
+    ga, ra, fa, st, r3,
     zsend, zrecv, gsend, grecv, rsend, rrecv, fsend, frecv, esend, erecv, lsem,
 ):
     shift = (shift0, shift1)
@@ -67,13 +65,12 @@
 
     sibling = device(z, xh, y, xl, 1 - core)
     diagonal = device(z, xh, y, 1 - xl, 1 - core)
-    beyond = device(z, 1 - xh, y, xl, core)
-    y_peer = [device(z, xh, (y + d) % 4, xl, core) for d in range(1, 4)]
+    plane_peer = [device(z, (xh + n % 2) % 2, (y + n // 2) % 4, xl, core) for n in range(8)]
     z_peer = [[device((z + d) % 8, xh, y, xl if r == 0 else 1 - xl, core) for r in range(2)] for d in range(8)]
     across = z_peer[0][1]
 
     barrier = pltpu.get_barrier_semaphore()
-    peers = [z_peer[d][r] for d in (4, 3, 5, 2, 6, 1, 7) for r in range(2)] + [beyond] + y_peer + [diagonal, across, sibling]
+    peers = [z_peer[d][r] for d in (4, 3, 5, 2, 6, 1, 7) for r in range(2)] + plane_peer[1:] + [diagonal, across, sibling]
     for peer in peers:
         pl.semaphore_signal(barrier, inc=1, device_id=peer, device_id_type=MESH)
 
@@ -240,60 +237,28 @@
             ordering[...], lefts[who], (((1,), (1,)), ((), ())), preferred_element_type=F32
         ).astype(BF16)
 
-    def a_block(y_):
-        rows = pl.ds(pl.multiple_of(y_ * 96, 96), 96)
+    def block(n):
+        rows = pl.ds(pl.multiple_of((y + n // 2) % 4 * 192 + (xh + n % 2) % 2 * 96, 96), 96)
         return jnp.dot(left_t[rows, :], right[...], preferred_element_type=F32)
 
-    def b_block(xh_):
-        rows = pl.ds(pl.multiple_of(384 + xh_ * 192, 192), 192)
-        return jnp.dot(left_t[rows, :], right[...], preferred_element_type=F32)
-
-    gb[...] = b_block(1 - xh).astype(BF16)
-    first_b = send(gb, rb, rsend, rrecv, 3, beyond)
-    first_a, second_b = [], []
-    for d in (2, 1, 3):
-        ga[d - 1] = a_block((y + d) % 4).astype(BF16)
-        first_a.append(send(ga.at[d - 1], ra.at[d - 1], rsend, rrecv, d - 1, y_peer[d - 1]))
-    ta[...] = a_block(y)
-    tb[...] = b_block(xh)
-
-    for copy in first_a:
+    first = []
+    for n in (5, 4, 3, 7, 1, 2, 6):
+        ga[n - 1] = block(n).astype(BF16)
+        first.append(send(ga.at[n - 1], ra.at[n - 1], rsend, rrecv, n - 1, plane_peer[n]))
+    total = block(0)
+    for copy in first:
         copy.wait_recv()
-    total = ta[...]
-    for d in range(3):
-        total = total + ra[d].astype(F32)
-    ta[...] = total
-    sa[...] = total.astype(BF16)
-    rows = pl.ds(pl.multiple_of((1 - xh) * 48, 48), 48)
-    second_a = send(sa.at[rows], qa, rsend, rrecv, 4, beyond)
-    first_b.wait_recv()
-    total = tb[...] + rb[...].astype(F32)
-    tb[...] = total
-    sb[...] = total.astype(BF16)
-    for d in (2, 1, 3):
-        rows = pl.ds(pl.multiple_of((y + d) % 4 * 48, 48), 48)
-        second_b.append(send(sb.at[rows], qb.at[d - 1], rsend, rrecv, d + 4, y_peer[d - 1]))
+    for n in range(7):
+        total = total + ra[n].astype(F32)
+    fa[0:96, :] = total
 
     third = {}
-
-    def ready(source, first):
-        for to in range(4):
-            rows = slice(to * 12, to * 12 + 16)
-            tail = source[rows, 256:384].astype(BF16)
-            for side in range(2):
-                st[first + to, side, :, 0:128] = source[rows, side * 128 : side * 128 + 128].astype(BF16)
-                st[first + to, side, :, 128:256] = tail
-
-    second_a.wait_recv()
-    fa[0:48, :] = ta[pl.ds(pl.multiple_of(xh * 48, 48), 48), :] + qa[...].astype(F32)
-    ready(fa, 0)
-    for copy in second_b:
-        copy.wait_recv()
-    total = tb[pl.ds(pl.multiple_of(y * 48, 48), 48), :]
-    for d in range(3):
-        total = total + qb[d].astype(F32)
-    fb[0:48, :] = total
-    ready(fb, 4)
+    for to in range(8):
+        rows = slice(to * 12, to * 12 + 16)
+        tail = fa[rows, 256:384].astype(BF16)
+        for side in range(2):
+            st[to, side, :, 0:128] = fa[rows, side * 128 : side * 128 + 128].astype(BF16)
+            st[to, side, :, 128:256] = tail
     for d in (4, 3, 5, 2, 6, 1, 7, 0):
         for r in range(2):
             if d or r:
@@ -347,18 +312,9 @@
             pltpu.VMEM((COLS, 2 * PAIRS), BF16),
             pltpu.VMEM((2 * PAIRS, OWN), BF16),
             pltpu.VMEM((2, PAIRS, COLS), BF16),
-            pltpu.VMEM((3, 96, OWN), BF16),
-            pltpu.VMEM((192, OWN), BF16),
-            pltpu.VMEM((3, 96, OWN), BF16),
-            pltpu.VMEM((192, OWN), BF16),
-            pltpu.VMEM((96, OWN), F32),
-            pltpu.VMEM((192, OWN), F32),
-            pltpu.VMEM((96, OWN), BF16),
-            pltpu.VMEM((192, OWN), BF16),
-            pltpu.VMEM((48, OWN), BF16),
-            pltpu.VMEM((3, 48, OWN), BF16),
-            pltpu.VMEM((64, OWN), F32),
-            pltpu.VMEM((64, OWN), F32),
+            pltpu.VMEM((7, 96, OWN), BF16),
+            pltpu.VMEM((7, 96, OWN), BF16),
+            pltpu.VMEM((112, OWN), F32),
             pltpu.VMEM((8, 2, 16, 256), BF16),
             pltpu.VMEM((8, 2, 16, 256), BF16),
             dma((9,)), dma((9,)), dma((18,)), dma((18,)), dma((8,)), dma((8,)), dma((16,)), dma((16,)), dma((1,)), dma((1,)), dma((10,)),

time: 47.8 us -> 47.2 us (0.987)
  Pallas kernels: 45.8 us -> 45.3 us
    pallas_call x1, Pallas kernels: 45.8 us -> 45.3 us  [per_device(): pl.pallas_call(kernel, out_shape=jax.ShapeDtypeStruct((2, 12, 192), F32),...]
where the time goes in v8:
time: 47.2 us; the launch traced here: 46.7 us
  Pallas kernels  45.3 us (96%)
  local copies, waits for them, and re-layouts  1.39 us (3%)
    pallas_call x1, Pallas kernels, per_device(): pl.pallas_call(kernel, out_shape=jax.ShapeDtypeStruct((2, 12, 192), F32),...  45.3 us
    pallas_call x1, local copies, waits for them, and re-layouts, per_device(): pl.pallas_call(kernel, out_shape=jax.ShapeDtypeStruct((2, 12, 192), F32),...  1.39 us

profile of v8, /device:TPU:1, one launch (start us, length us, event | category | flops | bytes accessed | tf_op | source)
XLA Modules:
  0.0 46.7 jit_solution(9379405352485912729)
XLA Ops:
  0.0 45.3 %shard_map.82 = f32[2,12,192]{2,1,0:T(8,128)} custom-call(bf16[1,8,4096]{2,1,0:T(8,128)(2,1)} %occ_hbm.1, bf16[1,64,4096]{2,1,0:T(8,128)(2,1)} %emp_hbm.1, bf16[1,8]{1,0:T(2,128)(2,1)} %oe_hbm.1, bf16[1,64]{1,0:T(2,128)(2,1)} %ee_hbm.1, s32[2,64]{1,0:T(2,128)} %partner_hbm.1, s32[3,2,384]{2,1,0:T(2,128)} %bitcast.1, s32[1,768]{1,0:T(1,128)} %constant.4.clone.order_hbm, ...), custom_call_target="tpu_custom_call" | custom-call | tf_op jit(solution)/shard_map/pallas_call | solution.py:287
  45.3 1.4 %copy.9 = f32[2,12,192]{2,0,1:T(2,128)} copy(f32[2,12,192]{2,1,0:T(8,128)} %shard_map.82) | data formatting | bytes 36864 | tf_op jit(solution)/shard_map/pallas_call | solution.py:287

commit v9 on v8

--- a/solution.py
+++ b/solution.py
@@ -242,7 +242,7 @@
         return jnp.dot(left_t[rows, :], right[...], preferred_element_type=F32)
 
     first = []
-    for n in (5, 4, 3, 7, 1, 2, 6):
+    for n in (5, 3, 7, 4, 1, 2, 6):
         ga[n - 1] = block(n).astype(BF16)
         first.append(send(ga.at[n - 1], ra.at[n - 1], rsend, rrecv, n - 1, plane_peer[n]))
     total = block(0)

time: 47.2 us -> 47.4 us (level)
  Pallas kernels: 45.3 us -> 45.8 us
where the time goes in v9:
time: 47.4 us; the launch traced here: 47.2 us
  Pallas kernels  45.8 us (97%)
  local copies, waits for them, and re-layouts  1.39 us (3%)
    pallas_call x1, Pallas kernels, per_device(): pl.pallas_call(kernel, out_shape=jax.ShapeDtypeStruct((2, 12, 192), F32),...  45.8 us
    pallas_call x1, local copies, waits for them, and re-layouts, per_device(): pl.pallas_call(kernel, out_shape=jax.ShapeDtypeStruct((2, 12, 192), F32),...  1.39 us

profile of v9, /device:TPU:1, one launch (start us, length us, event | category | flops | bytes accessed | tf_op | source)
XLA Modules:
  0.0 47.2 jit_solution(18385689009445109320)
XLA Ops:
  0.0 45.8 %shard_map.82 = f32[2,12,192]{2,1,0:T(8,128)} custom-call(bf16[1,8,4096]{2,1,0:T(8,128)(2,1)} %occ_hbm.1, bf16[1,64,4096]{2,1,0:T(8,128)(2,1)} %emp_hbm.1, bf16[1,8]{1,0:T(2,128)(2,1)} %oe_hbm.1, bf16[1,64]{1,0:T(2,128)(2,1)} %ee_hbm.1, s32[2,64]{1,0:T(2,128)} %partner_hbm.1, s32[3,2,384]{2,1,0:T(2,128)} %bitcast.1, s32[1,768]{1,0:T(1,128)} %constant.4.clone.order_hbm, ...), custom_call_target="tpu_custom_call" | custom-call | tf_op jit(solution)/shard_map/pallas_call | solution.py:287
  45.8 1.4 %copy.9 = f32[2,12,192]{2,0,1:T(2,128)} copy(f32[2,12,192]{2,1,0:T(8,128)} %shard_map.82) | data formatting | bytes 36864 | tf_op jit(solution)/shard_map/pallas_call | solution.py:287
